TPU v7x, 32 devices: a whole 2x2x4 slice. The times are simulated.
32 devices in a mesh: dp: 8 (over z, y), seq: 4 (over x, core).
Axes of the slice: x: 2, y: 2, z: 4, core: 2. Of those that a mesh axis runs over, the one named last changes fastest.
Arguments:
- sequence_in: bfloat16 [8, 2048, 768], P('dp', 'seq'), may hold values from -6 to 6
- output_grad: bfloat16 [8, 2048, 768], P('dp', 'seq'), may hold values from -6 to 6
- skip_mask: int32 [8, 2], P('dp'), may hold values 0 or 1
- in_gain: float32 [2, 768], replicated, may hold values from 0.25 to 1.75
- input_shift_vec: float32 [2, 768], replicated, may hold values from -3 to 3
- mid_gain: float32 [2, 384], replicated, may hold values from 0.25 to 1.75
- mid_offset: float32 [2, 384], replicated, may hold values from -3 to 3
- conv_weight: bfloat16 [2, 3, 768, 384], P(None, None, 'seq'), may hold values from -0.21875 to 0.21875
- point_weight: bfloat16 [384, 2, 768], P('seq'), may hold values from -0.3125 to 0.3125
Outputs:
- point_grad: float32 [384, 2, 768], P('seq')
- input_grad: bfloat16 [8, 2048, 768], P('dp', 'seq')
Inputs may be any that keep to these rules, and one draw needn't show every extreme that they name: skip_mask[s, b] = 1 means that sample s passes block b unchanged in this step.
All inputs are finite; a program needn't handle non-finite values.
Results may differ from a plain program's by a relative error of at most 0.009.
Values may be sent and summed in bfloat16 or wider, within the bound.
A program may use at most 64 MiB of HBM per device.

v0:
```python
import math

import jax
import jax.numpy as jnp
from jax import lax
from jax.sharding import PartitionSpec as P

FIRST_DILATION = 1024
SECOND_DILATION = 2048


def passed_along(value, axis, by):
    peers = lax.axis_size(axis)
    pairs = [(i, i + by) for i in range(peers) if 0 <= i + by < peers]
    return lax.ppermute(value, axis, pairs)


def gelu_tanh(values):
    return jax.nn.gelu(values, approximate=True)


def contract_last(left, right):
    return lax.dot_general(
        left, right, (((1,), (1,)), ((), ())), preferred_element_type=jnp.float32
    )


def neighbours(source, shards_away):
    if shards_away >= lax.axis_size("seq"):
        return (jnp.zeros_like(source), jnp.zeros_like(source))
    earlier = passed_along(source, "seq", shards_away)
    later = passed_along(source, "seq", -shards_away)
    return (earlier, later)


def forward_local(
    state, earlier, activated, later, weight, gain_vec, offset_vec, projection, kept_flag
):
    conv_out = jnp.dot(earlier, weight[0], preferred_element_type=jnp.float32)
    conv_out = conv_out + jnp.dot(activated, weight[1], preferred_element_type=jnp.float32)
    conv_out = conv_out + jnp.dot(later, weight[2], preferred_element_type=jnp.float32)
    middle = conv_out * gain_vec + offset_vec
    hidden_act = gelu_tanh(middle).astype(jnp.bfloat16)
    branch = jnp.dot(hidden_act, projection, preferred_element_type=jnp.float32)
    result = (state.astype(jnp.float32) + kept_flag * branch).astype(jnp.bfloat16)
    return (middle, hidden_act, result)


def backward_first(gradient, middle, projection, gain_vec, kept_flag):
    branch_grad = (kept_flag * gradient.astype(jnp.float32)).astype(jnp.bfloat16)
    hidden_grad = contract_last(branch_grad, projection)
    middle_grad = jax.vjp(gelu_tanh, middle)[1](hidden_grad)[0]
    conv_grad = (middle_grad * gain_vec).astype(jnp.bfloat16)
    return (conv_grad, branch_grad)


def backward_second(gradient, earlier, conv_grad, later, weight, normed, gain_vec):
    act_grad = (
        contract_last(later, weight[0])
        + contract_last(conv_grad, weight[1])
        + contract_last(earlier, weight[2])
    )
    normed_grad = jax.vjp(gelu_tanh, normed)[1](act_grad)[0] * gain_vec
    return (gradient.astype(jnp.float32) + normed_grad).astype(jnp.bfloat16)


def grad_rows(hidden_act, branch_grad):
    return lax.dot_general(
        hidden_act, branch_grad, (((0,), (0,)), ((), ())), preferred_element_type=jnp.float32
    )


def shards(
    sequence_in,
    output_grad,
    skip_mask,
    in_gain,
    input_shift_vec,
    mid_gain,
    mid_offset,
    conv_weight,
    point_weight,
):
    position_list = sequence_in.shape[1]
    channels = sequence_in.shape[2]
    point_full = lax.all_gather(point_weight, "seq", axis=0, tiled=True)
    neighbour_reach = (FIRST_DILATION // position_list, SECOND_DILATION // position_list)
    state = sequence_in.reshape(-1, channels)
    total_rows = state.shape[0]
    saved = []
    kept_weights = []
    for block_index in range(2):
        kept_flag = (1 - skip_mask[0, block_index]).astype(jnp.float32)
        normed = state.astype(jnp.float32) * in_gain[block_index] + input_shift_vec[block_index]
        activated = gelu_tanh(normed).astype(jnp.bfloat16)
        earlier, later = neighbours(
            activated.reshape(sequence_in.shape), neighbour_reach[block_index]
        )
        earlier = earlier.reshape(total_rows, channels)
        later = later.reshape(total_rows, channels)
        weight = lax.all_gather(conv_weight[block_index], "seq", axis=1, tiled=True)
        kept_weights.append(weight)
        operands = (
            state,
            earlier,
            activated,
            later,
            weight,
            mid_gain[block_index],
            mid_offset[block_index],
            point_full[:, block_index, :],
            kept_flag,
        )
        middle, hidden_act, state = forward_local(*operands)
        saved.append((normed, middle, hidden_act, kept_flag))
    gradient = output_grad.reshape(-1, channels)
    hidden_saved = [None, None]
    branch_saved = [None, None]
    for block_index in (1, 0):
        normed, middle, hidden_act, kept_flag = saved[block_index]
        projection = point_full[:, block_index, :]
        first_operands = (gradient, middle, projection, mid_gain[block_index], kept_flag)
        conv_grad, branch_grad = backward_first(*first_operands)
        hidden_saved[block_index] = hidden_act
        branch_saved[block_index] = branch_grad
        earlier, later = neighbours(
            conv_grad.reshape(sequence_in.shape[0], position_list, -1), neighbour_reach[block_index]
        )
        earlier = earlier.reshape(total_rows, -1)
        later = later.reshape(total_rows, -1)
        weight = lax.all_gather(conv_weight[block_index], "seq", axis=1, tiled=True)
        second_operands = (
            gradient,
            earlier,
            conv_grad,
            later,
            weight,
            normed,
            in_gain[block_index],
        )
        gradient = backward_second(*second_operands)
    first_term = grad_rows(hidden_saved[0], branch_saved[0])
    second_term = grad_rows(hidden_saved[1], branch_saved[1])
    shared_part = lax.psum_scatter(
        jnp.stack([first_term, second_term], axis=1), "seq", scatter_dimension=0, tiled=True
    )
    summed = lax.psum(shared_part, "dp")
    sample_count = sequence_in.shape[0] * lax.axis_size("dp")
    full_length = position_list * lax.axis_size("seq")
    point_grad = summed * (1.0 / math.sqrt(sample_count * full_length))
    return (point_grad, gradient.reshape(sequence_in.shape))


def solution(mesh):
    return jax.shard_map(
        shards,
        mesh=mesh,
        in_specs=(
            P("dp", "seq", None),
            P("dp", "seq", None),
            P("dp", None),
            P(),
            P(),
            P(),
            P(),
            P(None, None, "seq", None),
            P("seq", None, None),
        ),
        out_specs=(P("seq", None, None), P("dp", "seq", None)),
        check_vma=False,
    )
```

profile of v0, /device:TPU:0, one launch (start us, length us, event | category | flops | bytes accessed | tf_op | source)
XLA Modules:
  0.0 222.6 jit_solution(18223409144974421148)
XLA Ops:
  7.3 2.2 fusion.131
  9.6 0.7 all-gather.8.cloned.1.call-update
  10.3 0.7 copy.12
  11.9 1.3 collective-permute-start.1
  13.2 6.6 %collective-permute-start = (bf16[1,512,768]{2,1,0:T(8,128)(2,1)S(1)}, bf16[1,512,768]{2,1,0:T(8,128)(2,1)}, u32[]{:S(2)}, u32[]{:S(2)}) collective-permute-start(bf16[1,512,768]{2,1,0:T(8,128)(2,1)S(1)} %fusion.15), channel_id=1, source_target_pairs={{0,2},{1,3},{4,6},{5,7},{8,10},{9,11},{12,14},{13,15},{16,18},{17,... | collective-permute-start | bytes 2359304 | tf_op jit(solution)/shard_map/ppermute | solution.py:15
  21.7 21.5 %all-gather.10.cloned.1.call-done = bf16[1,3,768,384]{3,2,1,0:T(8,128)(2,1)} async-done(((bf16[1,3,192,384]{3,2,1,0:T(8,128)(2,1)}), bf16[1,3,768,384]{3,2,1,0:T(8,128)(2,1)}) %all-gather.10.cloned.1.call-update) | async-done | bytes 1769488 | tf_op jit(solution)/shard_map/all_gather | solution.py:131
  43.3 2.5 %fusion.93 = f32[512,384]{1,0:T(8,128)} fusion(bf16[1,3,768,384]{3,2,1,0:T(8,128)(2,1)} %all-gather.10.cloned.1.call-done), kind=kOutput, calls=%fused_computation.115 | convolution fusion | flops 301989888 | bytes 1376256 | tf_op jit(solution)/shard_map/dot_general | solution.py:39
  45.8 20.4 %all-gather.8.cloned.1.call-done = bf16[1,3,768,384]{3,2,1,0:T(8,128)(2,1)} async-done(((bf16[1,3,192,384]{3,2,1,0:T(8,128)(2,1)}), bf16[1,3,768,384]{3,2,1,0:T(8,128)(2,1)}) %all-gather.8.cloned.1.call-update) | async-done | bytes 1769488 | tf_op jit(solution)/shard_map/all_gather | solution.py:101
  66.2 1.8 fusion.66
  68.0 1.7 fusion.64
  69.7 1.7 fusion.43
  71.4 13.8 %all-gather.6.cloned.1.call-done = bf16[384,2,768]{2,0,1:T(8,128)(2,1)} async-done(((bf16[96,2,768]{2,0,1:T(8,128)(2,1)}), bf16[384,2,768]{2,0,1:T(8,128)(2,1)}) %all-gather.6.cloned.1.call-update) | async-done | bytes 1179664 | tf_op jit(solution)/shard_map/all_gather | solution.py:86
  85.3 1.9 fusion.4
  87.2 0.8 convolution_add_fusion.1
  88.7 0.9 copy-done.15
  89.5 0.7 convolution_bitcast_fusion
  90.2 4.2 %fusion.73 = f32[512,768]{1,0:T(8,128)} fusion(f32[512,384]{1,0:T(8,128)} %copy-done.15, bf16[1,512,768]{2,1,0:T(8,128)(2,1)} %param.10, f32[]{:T(128)} %bitcast.9, bf16[384,2,768]{2,0,1:T(8,128)(2,1)} %all-gather.6.cloned.1.call-done, bf16[1,3,768,384]{3,2,1,0:T(8,128)(2,1)} %all-gather.10.cloned.1.call-done, f32[384]{0:T(512)S(1)} %get-tuple-element.21), kind=kOutput, calls=%fused_computation.92 | convolution fusion | flops 609288192 | bytes 4327424 | tf_op jit(solution)/shard_map/dot_general | solution.py:23
  94.5 1.8 fusion.94
  96.3 3.3 %fusion.22 = bf16[512,768]{1,0:T(8,128)(2,1)S(1)} fusion(bf16[1,512,768]{2,1,0:T(8,128)(2,1)S(1)} %copy-done.14, f32[512,768]{1,0:T(8,128)S(1)} %fusion.94, f32[512,768]{1,0:T(8,128)} %fusion.73, bf16[512,768]{1,0:T(8,128)(2,1)S(1)} %copy-done.21, f32[768]{0:T(1024)S(1)} %get-tuple-element.8, f32[768]{0:T(1024)S(1)} %get-tuple-element.19, ...), kind=kOutput, calls=%fused_computation.34 | convolution fusion | flops 312999936 | bytes 6100992 | tf_op jit(solution)/shard_map/dot_general | solution.py:23
  99.6 0.7 convolution_bitcast_fusion.1
  100.4 1.6 pad_maximum_fusion
  102.1 1.1 copy-done.5
  103.4 2.7 %fusion.51 = bf16[512,384]{1,0:T(8,128)(2,1)} fusion(f32[512,384]{1,0:T(8,128)S(1)} %copy-done.5, bf16[512,768]{1,0:T(8,128)(2,1)S(1)} %copy-done.18, f32[]{:T(128)} %bitcast.6, bf16[384,2,768]{2,0,1:T(8,128)(2,1)} %all-gather.6.cloned.1.call-done, f32[384]{0:T(512)S(1)} %get-tuple-element.20), kind=kOutput, calls=%fused_computation.74 | convolution fusion | flops 307298304 | bytes 2557952 | tf_op jit(solution)/shard_map/dot_general | solution.py:23
  106.1 1.3 collective-permute-start.2
  107.4 6.0 %collective-permute-start.3 = (bf16[1,512,384]{2,1,0:T(8,128)(2,1)}, bf16[1,512,384]{2,1,0:T(8,128)(2,1)}, u32[]{:S(2)}, u32[]{:S(2)}) collective-permute-start(bf16[1,512,384]{2,1,0:T(8,128)(2,1)} %bitcast.18), channel_id=1, source_target_pairs={{0,2},{1,3},{4,6},{5,7},{8,10},{9,11},{12,14},{13,15},{16,18},{17,... | collective-permute-start | bytes 1179656 | tf_op jit(solution)/shard_map/ppermute | solution.py:15
  113.5 1.6 fusion.91
  115.1 20.2 %reduce-scatter.2.cloned.1.call-done = f32[96,2,768]{2,0,1:T(8,128)} async-done(((f32[384,2,768]{2,0,1:T(8,128)}), f32[96,2,768]{2,0,1:T(8,128)}) %reduce-scatter.2.cloned.1.call-update) | async-done | bytes 589840 | tf_op jit(solution)/shard_map/reduce_scatter | solution.py:144
  135.3 1.7 fusion.90
  137.1 3.5 %fusion.82 = bf16[1,512,768]{2,1,0:T(8,128)(2,1)} fusion(f32[768]{0:T(1024)S(1)} %get-tuple-element.9, f32[768]{0:T(1024)S(1)} %get-tuple-element.18, bf16[1,512,768]{2,1,0:T(8,128)(2,1)S(1)} %copy-done.2, f32[512,768]{1,0:T(8,128)S(1)} %fusion.90, f32[512,768]{1,0:T(8,128)S(1)} %fusion.91, bf16[512,768]{1,0:T(8,128)(2,1)S(1)} %copy-done.19, ...), kind=kOutput, calls=%fused_computation.100 | convolution fusion | flops 312999936 | bytes 6496256 | tf_op jit(solution)/shard_map/dot_general | solution.py:23
  140.6 73.1 %all-reduce.2.cloned.1.call-done = f32[96,2,768]{2,0,1:T(8,128)} async-done(((f32[96,2,768]{2,0,1:T(8,128)}), f32[96,2,768]{2,0,1:T(8,128)}) %all-reduce.2.cloned.1.call-update) | async-done | bytes 589840 | tf_op jit(solution)/shard_map/psum | solution.py:147
  213.7 1.1 broadcast_multiply_fusion
  214.8 1.3 copy.13
  (60 shorter events, 2.7 us)
Async XLA Ops:
  7.2 3.2 %copy-start.6 = (bf16[96,2,768]{2,1,0:T(2,128)(2,1)S(1)}, bf16[96,2,768]{2,1,0:T(2,128)(2,1)}, u32[]{:S(2)}) copy-start(bf16[96,2,768]{2,1,0:T(2,128)(2,1)} %param.17) | copy-start | bytes 884740
  7.2 4.0 %copy-start.9 = (f32[2,768]{1,0:T(2,128)S(1)}, f32[2,768]{1,0:T(2,128)}, u32[]{:S(2)}) copy-start(f32[2,768]{1,0:T(2,128)} %param.12) | copy-start | bytes 18436
  7.2 4.0 %copy-start.8 = (f32[2,768]{1,0:T(2,128)S(1)}, f32[2,768]{1,0:T(2,128)}, u32[]{:S(2)}) copy-start(f32[2,768]{1,0:T(2,128)} %param.13) | copy-start | bytes 18436
  7.2 4.0 %copy-start.1 = (bf16[1,512,768]{2,1,0:T(8,128)(2,1)S(1)}, bf16[1,512,768]{2,1,0:T(8,128)(2,1)}, u32[]{:S(2)}) copy-start(bf16[1,512,768]{2,1,0:T(8,128)(2,1)} %param.9) | copy-start | bytes 2359300
  7.2 36.1 %all-gather.10.cloned.1.call-start = ((), (), s32[]{:S(2)}) async-start(), calls=%async_computation.5 | async-start | bytes 2211840 | tf_op jit(solution)/shard_map/all_gather | solution.py:131
  9.5 10.3 %copy-start.12 = (s32[1,2]{1,0:T(1,128)S(1)}, s32[1,2]{1,0:T(1,128)}, u32[]{:S(2)}) copy-start(s32[1,2]{1,0:T(1,128)} %param.11) | copy-start | bytes 28
  9.5 12.2 %copy-start.10 = (f32[2,384]{1,0:T(2,128)S(1)}, f32[2,384]{1,0:T(2,128)}, u32[]{:S(2)}) copy-start(f32[2,384]{1,0:T(2,128)} %param.15) | copy-start | bytes 9220
  9.5 12.2 %copy-start.11 = (f32[2,384]{1,0:T(2,128)S(1)}, f32[2,384]{1,0:T(2,128)}, u32[]{:S(2)}) copy-start(f32[2,384]{1,0:T(2,128)} %param.14) | copy-start | bytes 9220
  9.5 56.7 %all-gather.8.cloned.1.call-start = ((), (), s32[]{:S(2)}) async-start(), calls=%async_computation.4 | async-start | bytes 2211840 | tf_op jit(solution)/shard_map/all_gather | solution.py:101
  10.3 75.0 %all-gather.6.cloned.1.call-start = ((), (), s32[]{:S(2)}) async-start(), calls=%async_computation.1 | async-start | bytes 1474560 | tf_op jit(solution)/shard_map/all_gather | solution.py:86
  11.1 124.2 %reduce-scatter.2.cloned.1.call-start = ((), (), s32[]{:S(2)}) async-start(), calls=%async_computation.2 | async-start | bytes 2949120 | tf_op jit(solution)/shard_map/reduce_scatter | solution.py:144
  11.9 56.1 %collective-permute-start.1 = (bf16[1,512,768]{2,1,0:T(8,128)(2,1)S(1)}, bf16[1,512,768]{2,1,0:T(8,128)(2,1)}, u32[]{:S(2)}, u32[]{:S(2)}) collective-permute-start(bf16[1,512,768]{2,1,0:T(8,128)(2,1)S(1)} %fusion.15), channel_id=1, source_target_pairs={{2,0},{3,1},{6,4},{7,5},{10,8},{11,9},{14,12},{15,13},{18,16},{19,... | collective-permute-start | bytes 2359304 | tf_op jit(solution)/shard_map/ppermute | solution.py:15
  13.2 56.5 %collective-permute-start = (bf16[1,512,768]{2,1,0:T(8,128)(2,1)S(1)}, bf16[1,512,768]{2,1,0:T(8,128)(2,1)}, u32[]{:S(2)}, u32[]{:S(2)}) collective-permute-start(bf16[1,512,768]{2,1,0:T(8,128)(2,1)S(1)} %fusion.15), channel_id=1, source_target_pairs={{0,2},{1,3},{4,6},{5,7},{8,10},{9,11},{12,14},{13,15},{16,18},{17,... | collective-permute-start | bytes 2359304 | tf_op jit(solution)/shard_map/ppermute | solution.py:15
  66.2 1.8 copy-start
  71.4 15.7 %copy-start.3 = (f32[512,384]{1,0:T(8,128)}, f32[512,384]{1,0:T(8,128)S(1)}, u32[]{:S(2)}) copy-start(f32[512,384]{1,0:T(8,128)S(1)} %fusion.43) | copy-start | bytes 2359300
  85.3 1.9 copy-start.7
  85.3 1.9 copy-start.16
  87.2 0.9 copy-start.20
  88.1 1.5 copy-start.13
  88.6 0.9 copy-start.15
  94.5 1.8 copy-start.14
  94.5 1.8 copy-start.21
  96.3 3.3 %copy-start.4 = (f32[512,384]{1,0:T(8,128)S(1)}, f32[512,384]{1,0:T(8,128)}, u32[]{:S(2)}) copy-start(f32[512,384]{1,0:T(8,128)} %copy-done.3) | copy-start | bytes 2359300
  99.6 0.9 copy-start.17
  102.0 1.1 copy-start.5
  102.0 1.4 copy-start.18
  102.0 111.6 %all-reduce.2.cloned.1.call-start = ((), (), s32[]{:S(2)}) async-start(), calls=%async_computation.3 | async-start | bytes 1179648 | tf_op jit(solution)/shard_map/psum | solution.py:147
  106.1 29.2 %collective-permute-start.2 = (bf16[1,512,384]{2,1,0:T(8,128)(2,1)}, bf16[1,512,384]{2,1,0:T(8,128)(2,1)}, u32[]{:S(2)}, u32[]{:S(2)}) collective-permute-start(bf16[1,512,384]{2,1,0:T(8,128)(2,1)} %bitcast.18), channel_id=1, source_target_pairs={{2,0},{3,1},{6,4},{7,5},{10,8},{11,9},{14,12},{15,13},{18,16},{19,... | collective-permute-start | bytes 1179656 | tf_op jit(solution)/shard_map/ppermute | solution.py:15
  107.4 29.6 %collective-permute-start.3 = (bf16[1,512,384]{2,1,0:T(8,128)(2,1)}, bf16[1,512,384]{2,1,0:T(8,128)(2,1)}, u32[]{:S(2)}, u32[]{:S(2)}) collective-permute-start(bf16[1,512,384]{2,1,0:T(8,128)(2,1)} %bitcast.18), channel_id=1, source_target_pairs={{0,2},{1,3},{4,6},{5,7},{8,10},{9,11},{12,14},{13,15},{16,18},{17,... | collective-permute-start | bytes 1179656 | tf_op jit(solution)/shard_map/ppermute | solution.py:15
  135.3 1.7 copy-start.2
  135.3 1.7 copy-start.19
Sparse Core Ops, SparseCore 0:
  10.2 33.0 all-gather.9
  45.4 20.7 all-gather.7
  67.8 17.4 all-gather.5
  102.2 33.0 reduce-scatter.1
  138.9 74.7 all-reduce.1
where the time goes:
time: 223 us
  waiting for transfers between devices  150 us (67%)
  matrix products  31.2 us (14%)
  starting transfers between devices  15.4 us (7%)
  between operations  15.4 us (7%)
  local copies, waits for them, and re-layouts  7.34 us (3%)
  other arithmetic  3.32 us (1%)
    psum x1, waiting for transfers between devices, shards(): summed = lax.psum(shared_part, 'dp')  73.1 us
    all_gather x2, waiting for transfers between devices, shards(): weight = lax.all_gather(conv_weight[block_index], 'seq', axis=1, tiled=True)  42 us
    reduce_scatter x1, waiting for transfers between devices, shards(): lax.psum_scatter(jnp.stack([first_term, second_term], axis=1), 'seq', sca...  20.2 us
    dot_general x7, matrix products, contract_last(): lax.dot_general(left, right, (((1,), (1,)), ((), ())), preferred_element_...  18.8 us
    ppermute x4, starting transfers between devices, passed_along(): return lax.ppermute(value, axis, pairs)  15.2 us
    all_gather x1, waiting for transfers between devices, shards(): point_full = lax.all_gather(point_weight, 'seq', axis=0, tiled=True)  13.8 us
  transfers between devices with their start and end apart: 9, of which 5 were waited for; matrix products, arithmetic and copies ran while one was open for 9% of the time, Pallas kernels for 0%

commit v1 on v0

--- a/solution.py
+++ b/solution.py
@@ -1,8 +1,11 @@
+import functools
 import math
 
 import jax
 import jax.numpy as jnp
 from jax import lax
+from jax.experimental import pallas as pl
+from jax.experimental.pallas import tpu as pltpu
 from jax.sharding import PartitionSpec as P
 
 FIRST_DILATION = 1024
@@ -70,6 +73,440 @@
     )
 
 
+MESH = pl.DeviceIdType.MESH
+CHUNKS = 4
+PIECES = 5
+TANH_SCALE = 0.7978845608028654
+CUBIC = 0.044715
+
+
+def gelu_and_slope(values):
+    squared = values * values
+    tanh = jnp.tanh(values * (TANH_SCALE + (TANH_SCALE * CUBIC) * squared))
+    gate = 0.5 + 0.5 * tanh
+    bend = values * (0.5 - 0.5 * tanh * tanh)
+    slope = gate + bend * (TANH_SCALE + (3.0 * TANH_SCALE * CUBIC) * squared)
+    return values * gate, slope
+
+
+def gelu_only(values):
+    tanh = jnp.tanh(values * (TANH_SCALE + (TANH_SCALE * CUBIC) * (values * values)))
+    return values * (0.5 + 0.5 * tanh)
+
+
+def dot(left, right):
+    return jnp.dot(left, right, preferred_element_type=jnp.float32)
+
+
+def paired_kernel(
+    x_ref,
+    og_ref,
+    skip_ref,
+    in_gain_ref,
+    in_shift_ref,
+    mid_gain_ref,
+    mid_offset_ref,
+    cw_ref,
+    pw_ref,
+    pg_ref,
+    gin_ref,
+    wbuf,
+    wpoint,
+    act0,
+    slope0,
+    own_conv,
+    hidden_grad1,
+    part_out,
+    part_in,
+    cgrad_out,
+    cgrad_in,
+    hidden0,
+    hidden1,
+    bgrad0,
+    bgrad1,
+    grad1,
+    term,
+    term_out,
+    core_in,
+    x_out,
+    x_in,
+    summed,
+    y_out,
+    y_in,
+    z_keep,
+    z_out,
+    z_in,
+    final,
+    ssem,
+    rsem,
+):
+    seq = lax.axis_index("seq")
+    dp = lax.axis_index("dp")
+    core = seq % 2
+    xpos = seq // 2
+    ypos = dp % 2
+    zpos = dp // 2
+    depth = z_in.shape[0]
+    core_mate = {"seq": seq + 1 - 2 * core}
+    x_mate = {"seq": (seq + 2) % 4}
+    y_mate = {"dp": dp + 1 - 2 * ypos}
+    z_mates = [{"dp": (dp + 2 * j) % (2 * depth)} for j in range(1, depth)]
+    rows = x_ref.shape[0]
+    size = rows // CHUNKS
+    channels = x_ref.shape[1]
+    hidden = own_conv.shape[1]
+    tap = 2 * xpos
+
+    barrier = pltpu.get_barrier_semaphore()
+    peers = [core_mate, x_mate, y_mate] + z_mates
+    for peer in peers:
+        pl.semaphore_signal(barrier, inc=1, device_id=peer, device_id_type=MESH)
+    pl.semaphore_wait(barrier, len(peers))
+
+    def remote(src, dst, index, peer):
+        return pltpu.make_async_remote_copy(
+            src_ref=src,
+            dst_ref=dst,
+            send_sem=ssem.at[index],
+            recv_sem=rsem.at[index],
+            device_id=peer,
+            device_id_type=MESH,
+        )
+
+    def mine(piece, for_mate):
+        if piece == 0:
+            return cw_ref.at[0, 2 - tap if for_mate else tap]
+        return (None, cw_ref.at[0, 1], pw_ref.at[0], cw_ref.at[1, 1], pw_ref.at[1])[piece]
+
+    def place(piece, owner):
+        where = (wbuf.at[0], wbuf.at[1], wpoint.at[0], wbuf.at[2], wpoint.at[1])[piece]
+        return where.at[owner]
+
+    far = (seq + 2) % 4
+    to_core, to_x, to_y, fwd_x, fwd_y = [], [], [], [], []
+    for k in range(PIECES):
+        to_core.append(remote(mine(k, False), place(k, seq), 5 * k, core_mate))
+        to_x.append(
+            remote(mine(k, True).at[ypos], place(k, seq).at[ypos], 5 * k + 1, x_mate)
+        )
+        half = place(k, far).at[ypos]
+        to_y.append(remote(half, half, 5 * k + 2, y_mate))
+        fwd_x.append(remote(half, half, 5 * k + 3, core_mate))
+        other = place(k, far).at[1 - ypos]
+        fwd_y.append(remote(other, other, 5 * k + 4, core_mate))
+    for k in range(PIECES):
+        to_x[k].start()
+        to_core[k].start()
+
+    def after_x(k):
+        to_x[k].wait_recv()
+        to_y[k].start()
+        fwd_x[k].start()
+
+    def after_y(k):
+        to_y[k].wait_recv()
+        fwd_y[k].start()
+
+    def ready(k):
+        to_core[k].wait_recv()
+        fwd_x[k].wait_recv()
+        fwd_y[k].wait_recv()
+
+    for k in range(PIECES):
+        place(k, seq)[...] = mine(k, False)[...]
+
+    keep = [(1 - skip_ref[0, b]).astype(jnp.float32) for b in range(2)]
+    in_gain = [in_gain_ref[b : b + 1, :] for b in range(2)]
+    in_shift = [in_shift_ref[b : b + 1, :] for b in range(2)]
+    mid_gain = [mid_gain_ref[b : b + 1, :] for b in range(2)]
+    mid_offset = [mid_offset_ref[b : b + 1, :] for b in range(2)]
+
+    def conv_full(k):
+        return wbuf[k].reshape(channels, hidden)
+
+    def point_full(b):
+        return wpoint[b].reshape(hidden, channels)
+
+    def at(r):
+        return pl.ds(pl.multiple_of(r * size, size), size)
+
+    def chunked(body):
+        def step(r, carry):
+            body(r)
+            return carry
+
+        lax.fori_loop(0, CHUNKS, step, 0)
+
+    def start_block(r):
+        spot = at(r)
+        value = x_ref[spot, :].astype(jnp.float32) * in_gain[0] + in_shift[0]
+        gelu, slope = gelu_and_slope(value)
+        act0[spot, :] = gelu.astype(jnp.bfloat16)
+        slope0[spot, :] = slope * in_gain[0]
+        bgrad1[spot, :] = (keep[1] * og_ref[spot, :].astype(jnp.float32)).astype(jnp.bfloat16)
+
+    chunked(start_block)
+
+    part_base = 5 * PIECES
+    cgrad_base = part_base + CHUNKS
+    term_base = cgrad_base + CHUNKS
+
+    def part_copy(r):
+        return remote(part_out.at[at(r)], part_in.at[at(r)], part_base + r, x_mate)
+
+    def cgrad_copy(r):
+        return remote(cgrad_out.at[at(r)], cgrad_in.at[at(r)], cgrad_base + r, x_mate)
+
+    after_x(0)
+    after_x(1)
+    after_y(0)
+    ready(0)
+
+    def make_part(r):
+        spot = at(r)
+        part_out[spot, :] = dot(act0[spot, :], conv_full(0)).astype(jnp.bfloat16)
+        part_copy(r).start()
+
+    chunked(make_part)
+    after_x(2)
+    after_y(1)
+    after_x(3)
+    after_y(2)
+    ready(1)
+
+    def make_own(r):
+        spot = at(r)
+        own_conv[spot, :] = dot(act0[spot, :], conv_full(1))
+
+    chunked(make_own)
+    after_x(4)
+    after_y(3)
+    after_y(4)
+    ready(4)
+
+    def make_hidden_grad(r):
+        spot = at(r)
+        hidden_grad1[spot, :] = contract_last(bgrad1[spot, :], point_full(1))
+
+    chunked(make_hidden_grad)
+    ready(2)
+    ready(3)
+
+    def middle_part(r):
+        spot = at(r)
+        part_copy(r).wait_recv()
+        conv = own_conv[spot, :] + part_in[spot, :].astype(jnp.float32)
+        gelu, mid_slope0 = gelu_and_slope(conv * mid_gain[0] + mid_offset[0])
+        act_hidden0 = gelu.astype(jnp.bfloat16)
+        hidden0[spot, :] = act_hidden0
+        branch = dot(act_hidden0, point_full(0))
+        state = (x_ref[spot, :].astype(jnp.float32) + keep[0] * branch).astype(jnp.bfloat16)
+        gelu, slope1 = gelu_and_slope(state.astype(jnp.float32) * in_gain[1] + in_shift[1])
+        conv = dot(gelu.astype(jnp.bfloat16), conv_full(2))
+        gelu, mid_slope1 = gelu_and_slope(conv * mid_gain[1] + mid_offset[1])
+        hidden1[spot, :] = gelu.astype(jnp.bfloat16)
+        conv_grad = (mid_slope1 * hidden_grad1[spot, :] * mid_gain[1]).astype(jnp.bfloat16)
+        act_grad = contract_last(conv_grad, conv_full(2))
+        gradient = (
+            og_ref[spot, :].astype(jnp.float32) + slope1 * act_grad * in_gain[1]
+        ).astype(jnp.bfloat16)
+        grad1[spot, :] = gradient
+        branch_grad = (keep[0] * gradient.astype(jnp.float32)).astype(jnp.bfloat16)
+        bgrad0[spot, :] = branch_grad
+        hidden_grad = contract_last(branch_grad, point_full(0))
+        cgrad_out[spot, :] = (mid_slope0 * hidden_grad * mid_gain[0]).astype(jnp.bfloat16)
+        cgrad_copy(r).start()
+
+    chunked(middle_part)
+
+    core_copy = [
+        remote(term_out.at[b, 1 - core], core_in.at[b], term_base + b, core_mate)
+        for b in range(2)
+    ]
+    x_copy = [remote(x_out.at[b], x_in.at[b], term_base + 2 + b, x_mate) for b in range(2)]
+    y_copy = remote(y_out, y_in, term_base + 4, y_mate)
+    z_copy = [
+        remote(z_out.at[(zpos + j) % depth], z_in.at[j], term_base + 4 + j, z_mates[j - 1])
+        for j in range(1, depth)
+    ]
+    gather_base = term_base + 4 + depth
+    own_quarter = final.at[ypos, zpos]
+    z_gather = [
+        remote(own_quarter, own_quarter, gather_base + j - 1, z_mates[j - 1])
+        for j in range(1, depth)
+    ]
+    y_gather = []
+    for j in range(depth):
+        quarter = final.at[ypos, (zpos + depth - j) % depth]
+        y_gather.append(remote(quarter, quarter, gather_base + depth - 1 + j, y_mate))
+
+    share = hidden // 4
+    for b, kept, branch in ((1, hidden1, bgrad1), (0, hidden0, bgrad0)):
+        product = grad_rows(kept[...], branch[...])
+        for owner in range(4):
+            block = product[owner * share : (owner + 1) * share, :]
+            term[b, owner % 2, owner // 2] = block
+            term_out[b, owner % 2, owner // 2] = block.astype(jnp.bfloat16)
+        core_copy[b].start()
+
+    def last_part(r):
+        spot = at(r)
+        cgrad_copy(r).wait_recv()
+        act_grad = contract_last(cgrad_out[spot, :], conv_full(1))
+        act_grad = act_grad + contract_last(cgrad_in[spot, :], conv_full(0))
+        gin_ref[spot, :] = (
+            grad1[spot, :].astype(jnp.float32) + slope0[spot, :] * act_grad
+        ).astype(jnp.bfloat16)
+
+    for b in (1, 0):
+        core_copy[b].wait_recv()
+        away = term[b, core, 1 - xpos] + core_in[b, 1 - xpos].astype(jnp.float32)
+        x_out[b] = away.astype(jnp.bfloat16)
+        x_copy[b].start()
+    last_part(0)
+    for b in (1, 0):
+        near = term[b, core, xpos] + core_in[b, xpos].astype(jnp.float32)
+        x_copy[b].wait_recv()
+        summed[b] = near + x_in[b].astype(jnp.float32)
+    y_out[...] = summed[1 - ypos].astype(jnp.bfloat16)
+    y_copy.start()
+    last_part(1)
+    y_copy.wait_recv()
+    half_rows, half_cols = z_keep.shape[1:]
+    whole = summed[ypos] + y_in[...].astype(jnp.float32)
+    for q in range(depth):
+        row, col = (q // 2) * half_rows, (q % 2) * half_cols
+        block = whole[row : row + half_rows, col : col + half_cols]
+        z_keep[q] = block
+        z_out[q] = block.astype(jnp.bfloat16)
+    for copy in z_copy:
+        copy.start()
+    last_part(2)
+    total = z_keep[zpos]
+    for j in range(1, depth):
+        z_copy[j - 1].wait_recv()
+        total = total + z_in[j].astype(jnp.float32)
+    final[ypos, zpos] = total.astype(jnp.bfloat16)
+    for copy in z_gather:
+        copy.start()
+    y_gather[0].start()
+    last_part(3)
+    for j in range(1, depth):
+        z_gather[j - 1].wait_recv()
+        y_gather[j].start()
+    for copy in y_gather:
+        copy.wait_recv()
+    for b in range(2):
+        for q in range(depth):
+            row, col = (q // 2) * half_rows, (q % 2) * half_cols
+            pg_ref[b, row : row + half_rows, col : col + half_cols] = final[b, q]
+
+    for group in (to_core, to_x, to_y, fwd_x, fwd_y, core_copy, x_copy, z_copy, z_gather, y_gather):
+        for copy in group:
+            copy.wait_send()
+    y_copy.wait_send()
+    for r in range(CHUNKS):
+        part_copy(r).wait_send()
+        cgrad_copy(r).wait_send()
+
+
+def paired_shards(
+    sequence_in,
+    output_grad,
+    skip_mask,
+    in_gain,
+    input_shift_vec,
+    mid_gain,
+    mid_offset,
+    conv_weight,
+    point_weight,
+):
+    rows, channels = sequence_in.shape[1:]
+    hidden = conv_weight.shape[3]
+    share = point_weight.shape[0]
+    depth = lax.axis_size("dp") // 2
+    taps = conv_weight.reshape(2, 3, 2, -1, hidden)
+    points = jnp.transpose(point_weight, (1, 0, 2)).reshape(2, 2, -1, channels)
+    taps_shape = taps.shape[2:]
+    points_shape = points.shape[1:]
+    copies = 5 * PIECES + 2 * CHUNKS + 5 + 3 * depth
+    vmem = pl.BlockSpec(memory_space=pltpu.VMEM)
+    bf16, f32 = jnp.bfloat16, jnp.float32
+    quarter = (share // 2, channels // 2)
+    scratch = [
+        pltpu.VMEM((3, 4) + taps_shape, bf16),
+        pltpu.VMEM((2, 4) + points_shape, bf16),
+        pltpu.VMEM((rows, channels), bf16),
+        pltpu.VMEM((rows, channels), f32),
+        pltpu.VMEM((rows, hidden), f32),
+        pltpu.VMEM((rows, hidden), f32),
+        pltpu.VMEM((rows, hidden), bf16),
+        pltpu.VMEM((rows, hidden), bf16),
+        pltpu.VMEM((rows, hidden), bf16),
+        pltpu.VMEM((rows, hidden), bf16),
+        pltpu.VMEM((rows, hidden), bf16),
+        pltpu.VMEM((rows, hidden), bf16),
+        pltpu.VMEM((rows, channels), bf16),
+        pltpu.VMEM((rows, channels), bf16),
+        pltpu.VMEM((rows, channels), bf16),
+        pltpu.VMEM((2, 2, 2, share, channels), f32),
+        pltpu.VMEM((2, 2, 2, share, channels), bf16),
+        pltpu.VMEM((2, 2, share, channels), bf16),
+        pltpu.VMEM((2, share, channels), bf16),
+        pltpu.VMEM((2, share, channels), bf16),
+        pltpu.VMEM((2, share, channels), f32),
+        pltpu.VMEM((share, channels), bf16),
+        pltpu.VMEM((share, channels), bf16),
+        pltpu.VMEM((depth,) + quarter, f32),
+        pltpu.VMEM((depth,) + quarter, bf16),
+        pltpu.VMEM((depth,) + quarter, bf16),
+        pltpu.VMEM((2, depth) + quarter, bf16),
+        pltpu.SemaphoreType.DMA((copies,)),
+        pltpu.SemaphoreType.DMA((copies,)),
+    ]
+    summed, gradient = pl.pallas_call(
+        paired_kernel,
+        out_shape=(
+            jax.ShapeDtypeStruct((2, share, channels), bf16),
+            jax.ShapeDtypeStruct((rows, channels), bf16),
+        ),
+        in_specs=[vmem, vmem, pl.BlockSpec(memory_space=pltpu.SMEM)] + [vmem] * 6,
+        out_specs=(vmem, vmem),
+        scratch_shapes=scratch,
+        compiler_params=pltpu.CompilerParams(
+            collective_id=0, has_side_effects=True, vmem_limit_bytes=48 * 2**20
+        ),
+    )(
+        sequence_in.reshape(rows, channels),
+        output_grad.reshape(rows, channels),
+        skip_mask,
+        in_gain,
+        input_shift_vec,
+        mid_gain,
+        mid_offset,
+        taps,
+        points,
+    )
+    sample_count = sequence_in.shape[0] * lax.axis_size("dp")
+    full_length = rows * lax.axis_size("seq")
+    scale = 1.0 / math.sqrt(sample_count * full_length)
+    point_grad = jnp.transpose(summed, (1, 0, 2)).astype(f32) * scale
+    return (point_grad, gradient.reshape(sequence_in.shape))
+
+
+def pairs_apply(sequence_in):
+    count, positions = sequence_in.shape[:2]
+    peers = lax.axis_size("seq")
+    reach = (FIRST_DILATION // positions, SECOND_DILATION // positions)
+    return (
+        count == 1
+        and peers == 4
+        and lax.axis_size("dp") == 8
+        and 2 * reach[0] == peers
+        and reach[1] >= peers
+    )
+
+
 def shards(
     sequence_in,
     output_grad,
@@ -81,6 +518,18 @@
     conv_weight,
     point_weight,
 ):
+    if pairs_apply(sequence_in):
+        return paired_shards(
+            sequence_in,
+            output_grad,
+            skip_mask,
+            in_gain,
+            input_shift_vec,
+            mid_gain,
+            mid_offset,
+            conv_weight,
+            point_weight,
+        )
     position_list = sequence_in.shape[1]
     channels = sequence_in.shape[2]
     point_full = lax.all_gather(point_weight, "seq", axis=0, tiled=True)

time: 223 us -> 69.9 us (0.31)
  waiting for transfers between devices: 150 us -> 0 us
  Pallas kernels: 0 us -> 61.6 us
  matrix products: 31.2 us -> 0 us
  starting transfers between devices: 15.4 us -> 0 us
  between operations: 15.4 us -> 0.73 us
  other arithmetic: 3.32 us -> 0.04 us
    psum x1 -> x0, waiting for transfers between devices: 73.1 us -> none  [shards(): summed = lax.psum(shared_part, 'dp')]
    pallas_call x0 -> x1, Pallas kernels: none -> 61.6 us  [paired_shards(): pl.pallas_call(paired_kernel, out_shape=(jax.ShapeDtypeStruct((2, share,...]
    all_gather x3 -> x0, waiting for transfers between devices: 55.8 us -> none  [the longest x2 42 us: shards(): weight = lax.all_gather(conv_weight[block_index], 'seq', axis=1, tiled=True)]
    dot_general x16 -> x0, matrix products: 31.2 us -> none  [the longest x7 18.8 us: contract_last(): lax.dot_general(left, right, (((1,), (1,)), ((), ())), preferred_element_...]
    reduce_scatter x1 -> x0, waiting for transfers between devices: 20.2 us -> none  [shards(): lax.psum_scatter(jnp.stack([first_term, second_term], axis=1), 'seq', sca...]
    ppermute x4 -> x0, starting transfers between devices: 15.2 us -> none  [passed_along(): return lax.ppermute(value, axis, pairs)]
    slice x4 -> x0, local copies, waits for them, and re-layouts: 2.88 us -> none  [the longest x1 2.22 us: shards(): weight = lax.all_gather(conv_weight[block_index], 'seq', axis=1, tiled=True)]
    unnamed x46 -> x18, local copies, waits for them, and re-layouts: 4.46 us -> 6.21 us
  transfers between devices with their start and end apart: 9 -> 0, of which waited for: 5 -> 0; matrix products, arithmetic and copies ran while one was open for 9% -> 0% of each run, Pallas kernels for 0% -> 0%
where the time goes in v1:
time: 69.9 us; the launch traced here: 69.6 us
  Pallas kernels  61.6 us (88%)
  local copies, waits for them, and re-layouts  7.23 us (10%)
  between operations  0.73 us (1%)
    pallas_call x1, Pallas kernels, paired_shards(): pl.pallas_call(paired_kernel, out_shape=(jax.ShapeDtypeStruct((2, share,...  61.6 us
    unnamed x18, local copies, waits for them, and re-layouts  6.21 us

profile of v1, /device:TPU:0, one launch (start us, length us, event | category | flops | bytes accessed | tf_op | source)
XLA Modules:
  0.0 69.6 jit_solution(14140903593984521406)
XLA Ops:
  0.6 0.0 copy-start.3
  0.6 0.0 copy-start.4
  0.7 0.0 copy-start.5
  0.7 0.0 copy-start.6
  0.7 1.0 %copy.11 = bf16[2,96,768]{2,1,0:T(8,128)(2,1)S(1)} copy(bf16[2,96,768]{2,0,1:T(2,128)(2,1)} %bitcast.13) | data formatting | bytes 589824 | tf_op jit(solution)/shard_map/transpose | solution.py:429
  1.7 0.0 copy-start.7
  1.7 0.0 copy-done.3
  1.7 0.0 copy-done.4
  1.7 0.0 copy-done.5
  1.7 0.0 copy-done.6
  1.7 0.6 copy-done.7
  2.3 0.0 copy-start
  2.4 1.2 %copy-done = bf16[2,3,192,384]{3,2,1,0:T(8,128)(2,1)S(1)} copy-done((bf16[2,3,192,384]{3,2,1,0:T(8,128)(2,1)S(1)}, bf16[2,3,192,384]{3,2,1,0:T(8,128)(2,1)}, u32[]{:S(2)}) %copy-start) | copy-done | bytes 884760
  3.5 0.0 copy-start.1
  3.5 1.1 %copy-done.1 = bf16[1,512,768]{2,1,0:T(8,128)(2,1)S(1)} copy-done((bf16[1,512,768]{2,1,0:T(8,128)(2,1)S(1)}, bf16[1,512,768]{2,1,0:T(8,128)(2,1)}, u32[]{:S(2)}) %copy-start.1) | copy-done | bytes 786456
  4.7 0.0 copy-start.2
  4.7 1.1 %copy-done.2 = bf16[1,512,768]{2,1,0:T(8,128)(2,1)S(1)} copy-done((bf16[1,512,768]{2,1,0:T(8,128)(2,1)S(1)}, bf16[1,512,768]{2,1,0:T(8,128)(2,1)}, u32[]{:S(2)}) %copy-start.2) | copy-done | bytes 786456
  5.8 61.6 %shard_map.104 = (bf16[2,96,768]{2,1,0:T(8,128)(2,1)S(1)}, bf16[512,768]{1,0:T(8,128)(2,1)S(1)}) custom-call(bf16[512,768]{1,0:T(8,128)(2,1)S(1)} %bitcast.11, bf16[512,768]{1,0:T(8,128)(2,1)S(1)} %bitcast.12, s32[1,2]{1,0:T(1,128)S(1)} %copy-done.7, f32[2,768]{1,0:T(2,128)S(1)} %copy-done.3, f32[2,768]{1,0:T(2,128)S(1)} %copy-done.4, ...), custom_call_target="tpu_custom_call" | custom-call | tf_op jit(solution)/shard_map/pallas_call | solution.py:467
  67.4 1.3 %copy.12 = f32[96,2,768]{2,1,0:T(2,128)} copy(f32[96,2,768]{2,0,1:T(8,128)S(1)} %multiply_bitcast_fusion) | data formatting | bytes 1179648
  68.7 0.9 %copy.14 = bf16[1,512,768]{2,1,0:T(8,128)(2,1)} copy(bf16[1,512,768]{2,1,0:T(8,128)(2,1)S(1)} %bitcast.10) | data formatting | bytes 1572864
  (1 shorter events, 0.0 us)
Async XLA Ops:
  0.6 1.1 %copy-start.3 = (f32[2,768]{1,0:T(2,128)S(1)}, f32[2,768]{1,0:T(2,128)}, u32[]{:S(2)}) copy-start(f32[2,768]{1,0:T(2,128)} %in_gain_ref.1) | copy-start | bytes 18436
  0.6 1.1 %copy-start.4 = (f32[2,768]{1,0:T(2,128)S(1)}, f32[2,768]{1,0:T(2,128)}, u32[]{:S(2)}) copy-start(f32[2,768]{1,0:T(2,128)} %in_shift_ref.1) | copy-start | bytes 18436
  0.7 1.1 %copy-start.5 = (f32[2,384]{1,0:T(2,128)S(1)}, f32[2,384]{1,0:T(2,128)}, u32[]{:S(2)}) copy-start(f32[2,384]{1,0:T(2,128)} %mid_gain_ref.1) | copy-start | bytes 9220
  0.7 1.1 %copy-start.6 = (f32[2,384]{1,0:T(2,128)S(1)}, f32[2,384]{1,0:T(2,128)}, u32[]{:S(2)}) copy-start(f32[2,384]{1,0:T(2,128)} %mid_offset_ref.1) | copy-start | bytes 9220
  1.7 0.7 copy-start.7
  2.3 1.2 %copy-start = (bf16[2,3,192,384]{3,2,1,0:T(8,128)(2,1)S(1)}, bf16[2,3,192,384]{3,2,1,0:T(8,128)(2,1)}, u32[]{:S(2)}) copy-start(bf16[2,3,192,384]{3,2,1,0:T(8,128)(2,1)} %param.16) | copy-start | bytes 2654212
  3.5 1.1 %copy-start.1 = (bf16[1,512,768]{2,1,0:T(8,128)(2,1)S(1)}, bf16[1,512,768]{2,1,0:T(8,128)(2,1)}, u32[]{:S(2)}) copy-start(bf16[1,512,768]{2,1,0:T(8,128)(2,1)} %param.9) | copy-start | bytes 2359300
  4.7 1.1 %copy-start.2 = (bf16[1,512,768]{2,1,0:T(8,128)(2,1)S(1)}, bf16[1,512,768]{2,1,0:T(8,128)(2,1)}, u32[]{:S(2)}) copy-start(bf16[1,512,768]{2,1,0:T(8,128)(2,1)} %param.10) | copy-start | bytes 2359300

commit v2 on v1

--- a/solution.py
+++ b/solution.py
@@ -74,7 +74,7 @@
 
 
 MESH = pl.DeviceIdType.MESH
-CHUNKS = 4
+CHUNKS = 2
 PIECES = 5
 TANH_SCALE = 0.7978845608028654
 CUBIC = 0.044715
@@ -99,8 +99,9 @@
 
 
 def paired_kernel(
-    x_ref,
-    og_ref,
+    scale,
+    x_hbm,
+    og_hbm,
     skip_ref,
     in_gain_ref,
     in_shift_ref,
@@ -110,6 +111,9 @@
     pw_ref,
     pg_ref,
     gin_ref,
+    x_ref,
+    og_ref,
+    points,
     wbuf,
     wpoint,
     act0,
@@ -128,17 +132,17 @@
     term,
     term_out,
     core_in,
+    y_out,
+    y_in,
     x_out,
     x_in,
-    summed,
-    y_out,
-    y_in,
     z_keep,
     z_out,
     z_in,
     final,
     ssem,
     rsem,
+    lsem,
 ):
     seq = lax.axis_index("seq")
     dp = lax.axis_index("dp")
@@ -161,6 +165,16 @@
     peers = [core_mate, x_mate, y_mate] + z_mates
     for peer in peers:
         pl.semaphore_signal(barrier, inc=1, device_id=peer, device_id_type=MESH)
+
+    def local(src, dst, index):
+        return pltpu.make_async_copy(src, dst, lsem.at[index])
+
+    load_x = local(x_hbm, x_ref, 0)
+    load_og = local(og_hbm, og_ref, 1)
+    load_x.start()
+    load_og.start()
+    for b in range(2):
+        points[b] = pw_ref[:, b, :].reshape(points.shape[1:])
     pl.semaphore_wait(barrier, len(peers))
 
     def remote(src, dst, index, peer):
@@ -176,7 +190,7 @@
     def mine(piece, for_mate):
         if piece == 0:
             return cw_ref.at[0, 2 - tap if for_mate else tap]
-        return (None, cw_ref.at[0, 1], pw_ref.at[0], cw_ref.at[1, 1], pw_ref.at[1])[piece]
+        return (None, cw_ref.at[0, 1], points.at[0], cw_ref.at[1, 1], points.at[1])[piece]
 
     def place(piece, owner):
         where = (wbuf.at[0], wbuf.at[1], wpoint.at[0], wbuf.at[2], wpoint.at[1])[piece]
@@ -186,6 +200,10 @@
     to_core, to_x, to_y, fwd_x, fwd_y = [], [], [], [], []
     for k in range(PIECES):
         to_core.append(remote(mine(k, False), place(k, seq), 5 * k, core_mate))
+        if k == 0:
+            to_x.append(remote(mine(k, True), place(k, seq), 1, x_mate))
+            fwd_x.append(remote(place(k, far), place(k, far), 3, core_mate))
+            continue
         to_x.append(
             remote(mine(k, True).at[ypos], place(k, seq).at[ypos], 5 * k + 1, x_mate)
         )
@@ -194,26 +212,28 @@
         fwd_x.append(remote(half, half, 5 * k + 3, core_mate))
         other = place(k, far).at[1 - ypos]
         fwd_y.append(remote(other, other, 5 * k + 4, core_mate))
+    own = [local(mine(k, False), place(k, seq), 2 + k) for k in range(PIECES)]
     for k in range(PIECES):
         to_x[k].start()
         to_core[k].start()
+        own[k].start()
 
     def after_x(k):
         to_x[k].wait_recv()
-        to_y[k].start()
         fwd_x[k].start()
+        if k > 0:
+            to_y[k - 1].start()
 
     def after_y(k):
-        to_y[k].wait_recv()
-        fwd_y[k].start()
+        to_y[k - 1].wait_recv()
+        fwd_y[k - 1].start()
 
     def ready(k):
+        own[k].wait()
         to_core[k].wait_recv()
         fwd_x[k].wait_recv()
-        fwd_y[k].wait_recv()
-
-    for k in range(PIECES):
-        place(k, seq)[...] = mine(k, False)[...]
+        if k > 0:
+            fwd_y[k - 1].wait_recv()
 
     keep = [(1 - skip_ref[0, b]).astype(jnp.float32) for b in range(2)]
     in_gain = [in_gain_ref[b : b + 1, :] for b in range(2)]
@@ -245,6 +265,8 @@
         slope0[spot, :] = slope * in_gain[0]
         bgrad1[spot, :] = (keep[1] * og_ref[spot, :].astype(jnp.float32)).astype(jnp.bfloat16)
 
+    load_x.wait()
+    load_og.wait()
     chunked(start_block)
 
     part_base = 5 * PIECES
@@ -259,7 +281,6 @@
 
     after_x(0)
     after_x(1)
-    after_y(0)
     ready(0)
 
     def make_part(r):
@@ -268,8 +289,8 @@
         part_copy(r).start()
 
     chunked(make_part)
+    after_y(1)
     after_x(2)
-    after_y(1)
     after_x(3)
     after_y(2)
     ready(1)
@@ -317,19 +338,37 @@
         cgrad_out[spot, :] = (mid_slope0 * hidden_grad * mid_gain[0]).astype(jnp.bfloat16)
         cgrad_copy(r).start()
 
-    chunked(middle_part)
+    share = hidden // 4
+    half_cols = channels // 2
+
+    def add_terms(r, b):
+        spot = slice(r * size, (r + 1) * size)
+        kept, branch = ((hidden0, bgrad0), (hidden1, bgrad1))[b]
+        product = grad_rows(kept[spot, :], branch[spot, :])
+        for owner in range(4):
+            for col in range(2):
+                block = product[
+                    owner * share : (owner + 1) * share, col * half_cols : (col + 1) * half_cols
+                ]
+                where = (b, owner % 2, col, owner // 2)
+                if r > 0:
+                    block = block + term[where]
+                term[where] = block
+                if r == CHUNKS - 1:
+                    term_out[where] = block.astype(jnp.bfloat16)
 
     core_copy = [
         remote(term_out.at[b, 1 - core], core_in.at[b], term_base + b, core_mate)
         for b in range(2)
     ]
-    x_copy = [remote(x_out.at[b], x_in.at[b], term_base + 2 + b, x_mate) for b in range(2)]
-    y_copy = remote(y_out, y_in, term_base + 4, y_mate)
+    y_copy = [remote(y_out.at[b], y_in.at[b], term_base + 2 + b, y_mate) for b in range(2)]
+    x_copy = [remote(x_out.at[b], x_in.at[b], term_base + 4 + b, x_mate) for b in range(2)]
+    z_base = term_base + 6
     z_copy = [
-        remote(z_out.at[(zpos + j) % depth], z_in.at[j], term_base + 4 + j, z_mates[j - 1])
+        remote(z_out.at[(zpos + j) % depth], z_in.at[j], z_base + j - 1, z_mates[j - 1])
         for j in range(1, depth)
     ]
-    gather_base = term_base + 4 + depth
+    gather_base = z_base + depth - 1
     own_quarter = final.at[ypos, zpos]
     z_gather = [
         remote(own_quarter, own_quarter, gather_base + j - 1, z_mates[j - 1])
@@ -340,15 +379,6 @@
         quarter = final.at[ypos, (zpos + depth - j) % depth]
         y_gather.append(remote(quarter, quarter, gather_base + depth - 1 + j, y_mate))
 
-    share = hidden // 4
-    for b, kept, branch in ((1, hidden1, bgrad1), (0, hidden0, bgrad0)):
-        product = grad_rows(kept[...], branch[...])
-        for owner in range(4):
-            block = product[owner * share : (owner + 1) * share, :]
-            term[b, owner % 2, owner // 2] = block
-            term_out[b, owner % 2, owner // 2] = block.astype(jnp.bfloat16)
-        core_copy[b].start()
-
     def last_part(r):
         spot = at(r)
         cgrad_copy(r).wait_recv()
@@ -358,30 +388,37 @@
             grad1[spot, :].astype(jnp.float32) + slope0[spot, :] * act_grad
         ).astype(jnp.bfloat16)
 
+    for r in range(CHUNKS):
+        middle_part(r)
+        for b in (1, 0):
+            add_terms(r, b)
+            if r == CHUNKS - 1:
+                core_copy[b].start()
+
     for b in (1, 0):
         core_copy[b].wait_recv()
-        away = term[b, core, 1 - xpos] + core_in[b, 1 - xpos].astype(jnp.float32)
-        x_out[b] = away.astype(jnp.bfloat16)
-        x_copy[b].start()
+        away = term[b, core, 1 - ypos] + core_in[b, 1 - ypos].astype(jnp.float32)
+        y_out[b] = away.astype(jnp.bfloat16)
+        y_copy[b].start()
     last_part(0)
     for b in (1, 0):
-        near = term[b, core, xpos] + core_in[b, xpos].astype(jnp.float32)
+        y_copy[b].wait_recv()
+        away = term[b, core, ypos, 1 - xpos] + core_in[b, ypos, 1 - xpos].astype(jnp.float32)
+        x_out[b] = (away + y_in[b, 1 - xpos].astype(jnp.float32)).astype(jnp.bfloat16)
+        x_copy[b].start()
+    last_part(1)
+    half_rows = share // 2
+    for b in (1, 0):
+        near = term[b, core, ypos, xpos] + core_in[b, ypos, xpos].astype(jnp.float32)
+        near = near + y_in[b, xpos].astype(jnp.float32)
         x_copy[b].wait_recv()
-        summed[b] = near + x_in[b].astype(jnp.float32)
-    y_out[...] = summed[1 - ypos].astype(jnp.bfloat16)
-    y_copy.start()
-    last_part(1)
-    y_copy.wait_recv()
-    half_rows, half_cols = z_keep.shape[1:]
-    whole = summed[ypos] + y_in[...].astype(jnp.float32)
-    for q in range(depth):
-        row, col = (q // 2) * half_rows, (q % 2) * half_cols
-        block = whole[row : row + half_rows, col : col + half_cols]
-        z_keep[q] = block
-        z_out[q] = block.astype(jnp.bfloat16)
+        near = near + x_in[b].astype(jnp.float32)
+        for part in range(2):
+            block = near[part * half_rows : (part + 1) * half_rows, :]
+            z_keep[2 * b + part] = block
+            z_out[2 * b + part] = block.astype(jnp.bfloat16)
     for copy in z_copy:
         copy.start()
-    last_part(2)
     total = z_keep[zpos]
     for j in range(1, depth):
         z_copy[j - 1].wait_recv()
@@ -390,21 +427,22 @@
     for copy in z_gather:
         copy.start()
     y_gather[0].start()
-    last_part(3)
     for j in range(1, depth):
         z_gather[j - 1].wait_recv()
         y_gather[j].start()
     for copy in y_gather:
         copy.wait_recv()
     for b in range(2):
-        for q in range(depth):
-            row, col = (q // 2) * half_rows, (q % 2) * half_cols
-            pg_ref[b, row : row + half_rows, col : col + half_cols] = final[b, q]
-
-    for group in (to_core, to_x, to_y, fwd_x, fwd_y, core_copy, x_copy, z_copy, z_gather, y_gather):
+        for part in range(2):
+            for col in range(2):
+                block = final[col, 2 * b + part].astype(jnp.float32) * scale
+                spot = slice(part * half_rows, (part + 1) * half_rows)
+                pg_ref[spot, b, col * half_cols : (col + 1) * half_cols] = block
+
+    sums = (core_copy, x_copy, y_copy, z_copy, z_gather, y_gather)
+    for group in (to_core, to_x, to_y, fwd_x, fwd_y) + sums:
         for copy in group:
             copy.wait_send()
-    y_copy.wait_send()
     for r in range(CHUNKS):
         part_copy(r).wait_send()
         cgrad_copy(r).wait_send()
@@ -426,14 +464,19 @@
     share = point_weight.shape[0]
     depth = lax.axis_size("dp") // 2
     taps = conv_weight.reshape(2, 3, 2, -1, hidden)
-    points = jnp.transpose(point_weight, (1, 0, 2)).reshape(2, 2, -1, channels)
     taps_shape = taps.shape[2:]
-    points_shape = points.shape[1:]
-    copies = 5 * PIECES + 2 * CHUNKS + 5 + 3 * depth
+    points_shape = (2, share // 2, channels)
+    copies = 5 * PIECES + 2 * CHUNKS + 6 + 3 * depth
     vmem = pl.BlockSpec(memory_space=pltpu.VMEM)
+    hbm = pl.BlockSpec(memory_space=pltpu.HBM)
+    smem = pl.BlockSpec(memory_space=pltpu.SMEM)
     bf16, f32 = jnp.bfloat16, jnp.float32
     quarter = (share // 2, channels // 2)
+    half = (share, channels // 2)
     scratch = [
+        pltpu.VMEM((rows, channels), bf16),
+        pltpu.VMEM((rows, channels), bf16),
+        pltpu.VMEM((2,) + points_shape, bf16),
         pltpu.VMEM((3, 4) + taps_shape, bf16),
         pltpu.VMEM((2, 4) + points_shape, bf16),
         pltpu.VMEM((rows, channels), bf16),
@@ -449,28 +492,31 @@
         pltpu.VMEM((rows, channels), bf16),
         pltpu.VMEM((rows, channels), bf16),
         pltpu.VMEM((rows, channels), bf16),
-        pltpu.VMEM((2, 2, 2, share, channels), f32),
-        pltpu.VMEM((2, 2, 2, share, channels), bf16),
-        pltpu.VMEM((2, 2, share, channels), bf16),
-        pltpu.VMEM((2, share, channels), bf16),
-        pltpu.VMEM((2, share, channels), bf16),
-        pltpu.VMEM((2, share, channels), f32),
-        pltpu.VMEM((share, channels), bf16),
-        pltpu.VMEM((share, channels), bf16),
+        pltpu.VMEM((2, 2, 2, 2) + half, f32),
+        pltpu.VMEM((2, 2, 2, 2) + half, bf16),
+        pltpu.VMEM((2, 2, 2) + half, bf16),
+        pltpu.VMEM((2, 2) + half, bf16),
+        pltpu.VMEM((2, 2) + half, bf16),
+        pltpu.VMEM((2,) + half, bf16),
+        pltpu.VMEM((2,) + half, bf16),
         pltpu.VMEM((depth,) + quarter, f32),
         pltpu.VMEM((depth,) + quarter, bf16),
         pltpu.VMEM((depth,) + quarter, bf16),
         pltpu.VMEM((2, depth) + quarter, bf16),
         pltpu.SemaphoreType.DMA((copies,)),
         pltpu.SemaphoreType.DMA((copies,)),
+        pltpu.SemaphoreType.DMA((2 + PIECES,)),
     ]
-    summed, gradient = pl.pallas_call(
-        paired_kernel,
+    sample_count = sequence_in.shape[0] * lax.axis_size("dp")
+    full_length = rows * lax.axis_size("seq")
+    scale = 1.0 / math.sqrt(sample_count * full_length)
+    point_grad, gradient = pl.pallas_call(
+        functools.partial(paired_kernel, scale),
         out_shape=(
-            jax.ShapeDtypeStruct((2, share, channels), bf16),
+            jax.ShapeDtypeStruct((share, 2, channels), f32),
             jax.ShapeDtypeStruct((rows, channels), bf16),
         ),
-        in_specs=[vmem, vmem, pl.BlockSpec(memory_space=pltpu.SMEM)] + [vmem] * 6,
+        in_specs=[hbm, hbm, smem] + [vmem] * 4 + [hbm, vmem],
         out_specs=(vmem, vmem),
         scratch_shapes=scratch,
         compiler_params=pltpu.CompilerParams(
@@ -485,12 +531,8 @@
         mid_gain,
         mid_offset,
         taps,
-        points,
+        point_weight,
     )
-    sample_count = sequence_in.shape[0] * lax.axis_size("dp")
-    full_length = rows * lax.axis_size("seq")
-    scale = 1.0 / math.sqrt(sample_count * full_length)
-    point_grad = jnp.transpose(summed, (1, 0, 2)).astype(f32) * scale
     return (point_grad, gradient.reshape(sequence_in.shape))
 
 

time: 69.9 us -> 67 us (0.959)
  Pallas kernels: 61.6 us -> 57.1 us
  local copies, waits for them, and re-layouts: 7.23 us -> 8.83 us
    pallas_call x1, Pallas kernels: 61.6 us -> 57.1 us  [paired_shards(): pl.pallas_call(functools.partial(paired_kernel, scale), out_shape=(jax.Sh...]
    unnamed x18 -> x20, local copies, waits for them, and re-layouts: 6.21 us -> 8.83 us
    transpose x1 -> x0, local copies, waits for them, and re-layouts: 1.02 us -> none  [paired_shards(): points = jnp.transpose(point_weight, (1, 0, 2)).reshape(2, 2, -1, channels)]
where the time goes in v2:
time: 67 us; the launch traced here: 66.6 us
  Pallas kernels  57.1 us (85%)
  local copies, waits for them, and re-layouts  8.83 us (13%)
  between operations  0.67 us (1%)
    pallas_call x1, Pallas kernels, paired_shards(): pl.pallas_call(functools.partial(paired_kernel, scale), out_shape=(jax.Sh...  57.1 us
    unnamed x20, local copies, waits for them, and re-layouts  8.83 us

profile of v2, /device:TPU:0, one launch (start us, length us, event | category | flops | bytes accessed | tf_op | source)
XLA Modules:
  0.0 66.6 jit_solution(1628599301964258485)
XLA Ops:
  0.6 0.0 copy-start.6
  0.6 0.0 copy-start.8
  0.7 0.7 copy-done.6
  1.3 0.0 copy-done.8
  1.3 0.0 copy-start
  1.3 1.2 %copy-done = bf16[2,3,192,384]{3,2,1,0:T(8,128)(2,1)S(1)} copy-done((bf16[2,3,192,384]{3,2,1,0:T(8,128)(2,1)S(1)}, bf16[2,3,192,384]{3,2,1,0:T(8,128)(2,1)}, u32[]{:S(2)}) %copy-start) | copy-done | bytes 884760
  2.5 0.0 copy-start.1
  2.5 1.1 %copy-done.1 = bf16[1,512,768]{2,1,0:T(8,128)(2,1)S(1)} copy-done((bf16[1,512,768]{2,1,0:T(8,128)(2,1)S(1)}, bf16[1,512,768]{2,1,0:T(8,128)(2,1)}, u32[]{:S(2)}) %copy-start.1) | copy-done | bytes 786456
  3.6 0.0 copy-start.2
  3.6 1.1 %copy-done.2 = bf16[1,512,768]{2,1,0:T(8,128)(2,1)S(1)} copy-done((bf16[1,512,768]{2,1,0:T(8,128)(2,1)S(1)}, bf16[1,512,768]{2,1,0:T(8,128)(2,1)}, u32[]{:S(2)}) %copy-start.2) | copy-done | bytes 786456
  4.8 0.0 copy-start.3
  4.8 1.0 %copy-done.3 = bf16[96,2,768]{2,1,0:T(2,128)(2,1)S(1)} copy-done((bf16[96,2,768]{2,1,0:T(2,128)(2,1)S(1)}, bf16[96,2,768]{2,1,0:T(2,128)(2,1)}, u32[]{:S(2)}) %copy-start.3) | copy-done | bytes 294936
  5.7 0.0 copy-start.4
  5.7 0.7 %copy-done.4 = f32[2,768]{1,0:T(2,128)S(1)} copy-done((f32[2,768]{1,0:T(2,128)S(1)}, f32[2,768]{1,0:T(2,128)}, u32[]{:S(2)}) %copy-start.4) | copy-done | bytes 6168
  6.4 0.0 copy-start.5
  6.4 0.7 %copy-done.5 = f32[2,768]{1,0:T(2,128)S(1)} copy-done((f32[2,768]{1,0:T(2,128)S(1)}, f32[2,768]{1,0:T(2,128)}, u32[]{:S(2)}) %copy-start.5) | copy-done | bytes 6168
  7.1 0.0 copy-start.7
  7.1 0.7 %copy-done.7 = f32[2,384]{1,0:T(2,128)S(1)} copy-done((f32[2,384]{1,0:T(2,128)S(1)}, f32[2,384]{1,0:T(2,128)}, u32[]{:S(2)}) %copy-start.7) | copy-done | bytes 3096
  7.8 57.1 %shard_map.104 = (f32[96,2,768]{2,1,0:T(2,128)S(1)}, bf16[512,768]{1,0:T(8,128)(2,1)S(1)}) custom-call(bf16[512,768]{1,0:T(8,128)(2,1)S(1)} %bitcast.6, bf16[512,768]{1,0:T(8,128)(2,1)S(1)} %bitcast.7, s32[1,2]{1,0:T(1,128)S(1)} %copy-done.8, f32[2,768]{1,0:T(2,128)S(1)} %copy-done.4, f32[2,768]{1,0:T(2,128)S(1)} %copy-done.5, f32[2,384]{1,0:T(2,128)S(1)} %copy-done.6, ...), custom_call_target="tpu_custom_call" | custom-call | tf_op jit(solution)/shard_map/pallas_call | solution.py:513
  64.9 0.8 %copy.13 = f32[96,2,768]{2,1,0:T(2,128)} copy(f32[96,2,768]{2,1,0:T(2,128)S(1)} %get-tuple-element.8) | data formatting | bytes 1179648
  65.7 0.9 %copy.14 = bf16[1,512,768]{2,1,0:T(8,128)(2,1)} copy(bf16[1,512,768]{2,1,0:T(8,128)(2,1)S(1)} %bitcast.5) | data formatting | bytes 1572864
Async XLA Ops:
  0.6 0.7 %copy-start.6 = (f32[2,384]{1,0:T(2,128)S(1)}, f32[2,384]{1,0:T(2,128)}, u32[]{:S(2)}) copy-start(f32[2,384]{1,0:T(2,128)} %mid_gain_ref.1) | copy-start | bytes 9220
  0.6 0.7 %copy-start.8 = (s32[1,2]{1,0:T(1,128)S(1)}, s32[1,2]{1,0:T(1,128)}, u32[]{:S(2)}) copy-start(s32[1,2]{1,0:T(1,128)} %skip_ref.1) | copy-start | bytes 28
  1.3 1.2 %copy-start = (bf16[2,3,192,384]{3,2,1,0:T(8,128)(2,1)S(1)}, bf16[2,3,192,384]{3,2,1,0:T(8,128)(2,1)}, u32[]{:S(2)}) copy-start(bf16[2,3,192,384]{3,2,1,0:T(8,128)(2,1)} %param.16) | copy-start | bytes 2654212
  2.5 1.1 %copy-start.1 = (bf16[1,512,768]{2,1,0:T(8,128)(2,1)S(1)}, bf16[1,512,768]{2,1,0:T(8,128)(2,1)}, u32[]{:S(2)}) copy-start(bf16[1,512,768]{2,1,0:T(8,128)(2,1)} %param.9) | copy-start | bytes 2359300
  3.6 1.1 %copy-start.2 = (bf16[1,512,768]{2,1,0:T(8,128)(2,1)S(1)}, bf16[1,512,768]{2,1,0:T(8,128)(2,1)}, u32[]{:S(2)}) copy-start(bf16[1,512,768]{2,1,0:T(8,128)(2,1)} %param.10) | copy-start | bytes 2359300
  4.8 1.0 %copy-start.3 = (bf16[96,2,768]{2,1,0:T(2,128)(2,1)S(1)}, bf16[96,2,768]{2,1,0:T(2,128)(2,1)}, u32[]{:S(2)}) copy-start(bf16[96,2,768]{2,1,0:T(2,128)(2,1)} %pw_ref.1) | copy-start | bytes 884740
  5.7 0.7 %copy-start.4 = (f32[2,768]{1,0:T(2,128)S(1)}, f32[2,768]{1,0:T(2,128)}, u32[]{:S(2)}) copy-start(f32[2,768]{1,0:T(2,128)} %in_gain_ref.1) | copy-start | bytes 18436
  6.4 0.7 %copy-start.5 = (f32[2,768]{1,0:T(2,128)S(1)}, f32[2,768]{1,0:T(2,128)}, u32[]{:S(2)}) copy-start(f32[2,768]{1,0:T(2,128)} %in_shift_ref.1) | copy-start | bytes 18436
  7.1 0.7 %copy-start.7 = (f32[2,384]{1,0:T(2,128)S(1)}, f32[2,384]{1,0:T(2,128)}, u32[]{:S(2)}) copy-start(f32[2,384]{1,0:T(2,128)} %mid_offset_ref.1) | copy-start | bytes 9220

commit v3 on v2

--- a/solution.py
+++ b/solution.py
@@ -103,11 +103,18 @@
     x_hbm,
     og_hbm,
     skip_ref,
+    in_gain_hbm,
+    in_shift_hbm,
+    mid_gain_hbm,
+    mid_offset_hbm,
+    cw_ref,
+    pw_hbm,
+    pg_hbm,
+    gin_hbm,
     in_gain_ref,
     in_shift_ref,
     mid_gain_ref,
     mid_offset_ref,
-    cw_ref,
     pw_ref,
     pg_ref,
     gin_ref,
@@ -132,10 +139,10 @@
     term,
     term_out,
     core_in,
-    y_out,
-    y_in,
-    x_out,
-    x_in,
+    one_out,
+    one_in,
+    two_out,
+    two_in,
     z_keep,
     z_out,
     z_in,
@@ -169,12 +176,18 @@
     def local(src, dst, index):
         return pltpu.make_async_copy(src, dst, lsem.at[index])
 
-    load_x = local(x_hbm, x_ref, 0)
-    load_og = local(og_hbm, og_ref, 1)
-    load_x.start()
-    load_og.start()
-    for b in range(2):
-        points[b] = pw_ref[:, b, :].reshape(points.shape[1:])
+    load_points = local(pw_hbm, pw_ref, 0)
+    loads = [
+        local(x_hbm, x_ref, 1),
+        local(og_hbm, og_ref, 2),
+        local(in_gain_hbm, in_gain_ref, 3),
+        local(in_shift_hbm, in_shift_ref, 4),
+        local(mid_gain_hbm, mid_gain_ref, 5),
+        local(mid_offset_hbm, mid_offset_ref, 6),
+    ]
+    load_points.start()
+    for load in loads:
+        load.start()
     pl.semaphore_wait(barrier, len(peers))
 
     def remote(src, dst, index, peer):
@@ -197,32 +210,55 @@
         return where.at[owner]
 
     far = (seq + 2) % 4
-    to_core, to_x, to_y, fwd_x, fwd_y = [], [], [], [], []
+    zlow = zpos % 2
+    z_near = {"dp": dp + 2 - 4 * zlow}
+
+    def quarter_of(half, which):
+        if half.shape[1] == hidden:
+            count = half.shape[0] // 2
+            return half.at[pl.ds(pl.multiple_of(which * count, count), count)]
+        count = half.shape[1] // 2
+        return half.at[:, pl.ds(pl.multiple_of(which * count, count), count)]
+
+    to_core, to_x, to_z, to_y, fwd_x, fwd_y = [], [], [], [], [], []
     for k in range(PIECES):
-        to_core.append(remote(mine(k, False), place(k, seq), 5 * k, core_mate))
+        to_core.append(remote(mine(k, False), place(k, seq), 6 * k, core_mate))
         if k == 0:
             to_x.append(remote(mine(k, True), place(k, seq), 1, x_mate))
             fwd_x.append(remote(place(k, far), place(k, far), 3, core_mate))
             continue
+        near_quarter = quarter_of(mine(k, True).at[ypos], zlow)
         to_x.append(
-            remote(mine(k, True).at[ypos], place(k, seq).at[ypos], 5 * k + 1, x_mate)
+            remote(near_quarter, quarter_of(place(k, seq).at[ypos], zlow), 6 * k + 1, x_mate)
         )
         half = place(k, far).at[ypos]
-        to_y.append(remote(half, half, 5 * k + 2, y_mate))
-        fwd_x.append(remote(half, half, 5 * k + 3, core_mate))
+        quarter = quarter_of(half, zlow)
+        to_z.append(remote(quarter, quarter, 6 * k + 5, z_near))
+        to_y.append(remote(half, half, 6 * k + 2, y_mate))
+        fwd_x.append(remote(half, half, 6 * k + 3, core_mate))
         other = place(k, far).at[1 - ypos]
-        fwd_y.append(remote(other, other, 5 * k + 4, core_mate))
-    own = [local(mine(k, False), place(k, seq), 2 + k) for k in range(PIECES)]
+        fwd_y.append(remote(other, other, 6 * k + 4, core_mate))
+    own = [local(mine(k, False), place(k, seq), 7 + k) for k in range(PIECES)]
     for k in range(PIECES):
+        if k == 2:
+            load_points.wait()
+            for b in range(2):
+                points[b] = pw_ref[:, b, :].reshape(points.shape[1:])
         to_x[k].start()
         to_core[k].start()
         own[k].start()
 
     def after_x(k):
         to_x[k].wait_recv()
+        if k == 0:
+            fwd_x[0].start()
+        else:
+            to_z[k - 1].start()
+
+    def after_z(k):
+        to_z[k - 1].wait_recv()
+        to_y[k - 1].start()
         fwd_x[k].start()
-        if k > 0:
-            to_y[k - 1].start()
 
     def after_y(k):
         to_y[k - 1].wait_recv()
@@ -235,6 +271,8 @@
         if k > 0:
             fwd_y[k - 1].wait_recv()
 
+    for load in loads:
+        load.wait()
     keep = [(1 - skip_ref[0, b]).astype(jnp.float32) for b in range(2)]
     in_gain = [in_gain_ref[b : b + 1, :] for b in range(2)]
     in_shift = [in_shift_ref[b : b + 1, :] for b in range(2)]
@@ -265,11 +303,9 @@
         slope0[spot, :] = slope * in_gain[0]
         bgrad1[spot, :] = (keep[1] * og_ref[spot, :].astype(jnp.float32)).astype(jnp.bfloat16)
 
-    load_x.wait()
-    load_og.wait()
     chunked(start_block)
 
-    part_base = 5 * PIECES
+    part_base = 6 * PIECES
     cgrad_base = part_base + CHUNKS
     term_base = cgrad_base + CHUNKS
 
@@ -281,6 +317,7 @@
 
     after_x(0)
     after_x(1)
+    after_x(2)
     ready(0)
 
     def make_part(r):
@@ -289,10 +326,11 @@
         part_copy(r).start()
 
     chunked(make_part)
+    after_x(3)
+    after_x(4)
+    for k in range(1, PIECES):
+        after_z(k)
     after_y(1)
-    after_x(2)
-    after_x(3)
-    after_y(2)
     ready(1)
 
     def make_own(r):
@@ -300,9 +338,8 @@
         own_conv[spot, :] = dot(act0[spot, :], conv_full(1))
 
     chunked(make_own)
-    after_x(4)
-    after_y(3)
-    after_y(4)
+    for k in range(2, PIECES):
+        after_y(k)
     ready(4)
 
     def make_hidden_grad(r):
@@ -336,7 +373,8 @@
         bgrad0[spot, :] = branch_grad
         hidden_grad = contract_last(branch_grad, point_full(0))
         cgrad_out[spot, :] = (mid_slope0 * hidden_grad * mid_gain[0]).astype(jnp.bfloat16)
-        cgrad_copy(r).start()
+        if r < CHUNKS - 1:
+            cgrad_copy(r).start()
 
     share = hidden // 4
     half_cols = channels // 2
@@ -350,7 +388,8 @@
                 block = product[
                     owner * share : (owner + 1) * share, col * half_cols : (col + 1) * half_cols
                 ]
-                where = (b, owner % 2, col, owner // 2)
+                first, second = (col, owner // 2) if b == 1 else (owner // 2, col)
+                where = (b, owner % 2, first, second)
                 if r > 0:
                     block = block + term[where]
                 term[where] = block
@@ -361,8 +400,9 @@
         remote(term_out.at[b, 1 - core], core_in.at[b], term_base + b, core_mate)
         for b in range(2)
     ]
-    y_copy = [remote(y_out.at[b], y_in.at[b], term_base + 2 + b, y_mate) for b in range(2)]
-    x_copy = [remote(x_out.at[b], x_in.at[b], term_base + 4 + b, x_mate) for b in range(2)]
+    ways = ((xpos, ypos, x_mate, y_mate), (ypos, xpos, y_mate, x_mate))
+    one_copy = [remote(one_out.at[b], one_in.at[b], term_base + 2 + b, ways[b][2]) for b in range(2)]
+    two_copy = [remote(two_out.at[b], two_in.at[b], term_base + 4 + b, ways[b][3]) for b in range(2)]
     z_base = term_base + 6
     z_copy = [
         remote(z_out.at[(zpos + j) % depth], z_in.at[j], z_base + j - 1, z_mates[j - 1])
@@ -387,6 +427,10 @@
         gin_ref[spot, :] = (
             grad1[spot, :].astype(jnp.float32) + slope0[spot, :] * act_grad
         ).astype(jnp.bfloat16)
+        gin_copy(r).start()
+
+    def gin_copy(r):
+        return local(gin_ref.at[at(r)], gin_hbm.at[at(r)], 7 + PIECES + r)
 
     for r in range(CHUNKS):
         middle_part(r)
@@ -396,29 +440,35 @@
                 core_copy[b].start()
 
     for b in (1, 0):
+        first = ways[b][0]
         core_copy[b].wait_recv()
-        away = term[b, core, 1 - ypos] + core_in[b, 1 - ypos].astype(jnp.float32)
-        y_out[b] = away.astype(jnp.bfloat16)
-        y_copy[b].start()
+        away = term[b, core, 1 - first] + core_in[b, 1 - first].astype(jnp.float32)
+        one_out[b] = away.astype(jnp.bfloat16)
+        one_copy[b].start()
     last_part(0)
     for b in (1, 0):
-        y_copy[b].wait_recv()
-        away = term[b, core, ypos, 1 - xpos] + core_in[b, ypos, 1 - xpos].astype(jnp.float32)
-        x_out[b] = (away + y_in[b, 1 - xpos].astype(jnp.float32)).astype(jnp.bfloat16)
-        x_copy[b].start()
-    last_part(1)
+        first, second = ways[b][:2]
+        one_copy[b].wait_recv()
+        away = term[b, core, first, 1 - second]
+        away = away + core_in[b, first, 1 - second].astype(jnp.float32)
+        away = away + one_in[b, 1 - second].astype(jnp.float32)
+        two_out[b] = away.astype(jnp.bfloat16)
+        two_copy[b].start()
+    cgrad_copy(CHUNKS - 1).start()
     half_rows = share // 2
     for b in (1, 0):
-        near = term[b, core, ypos, xpos] + core_in[b, ypos, xpos].astype(jnp.float32)
-        near = near + y_in[b, xpos].astype(jnp.float32)
-        x_copy[b].wait_recv()
-        near = near + x_in[b].astype(jnp.float32)
+        first, second = ways[b][:2]
+        near = term[b, core, first, second] + core_in[b, first, second].astype(jnp.float32)
+        near = near + one_in[b, second].astype(jnp.float32)
+        two_copy[b].wait_recv()
+        near = near + two_in[b].astype(jnp.float32)
         for part in range(2):
             block = near[part * half_rows : (part + 1) * half_rows, :]
             z_keep[2 * b + part] = block
             z_out[2 * b + part] = block.astype(jnp.bfloat16)
     for copy in z_copy:
         copy.start()
+    last_part(1)
     total = z_keep[zpos]
     for j in range(1, depth):
         z_copy[j - 1].wait_recv()
@@ -439,13 +489,17 @@
                 spot = slice(part * half_rows, (part + 1) * half_rows)
                 pg_ref[spot, b, col * half_cols : (col + 1) * half_cols] = block
 
-    sums = (core_copy, x_copy, y_copy, z_copy, z_gather, y_gather)
-    for group in (to_core, to_x, to_y, fwd_x, fwd_y) + sums:
+    pg_copy = local(pg_ref, pg_hbm, 7 + PIECES + CHUNKS)
+    pg_copy.start()
+    sums = (core_copy, one_copy, two_copy, z_copy, z_gather, y_gather)
+    for group in (to_core, to_x, to_z, to_y, fwd_x, fwd_y) + sums:
         for copy in group:
             copy.wait_send()
     for r in range(CHUNKS):
         part_copy(r).wait_send()
         cgrad_copy(r).wait_send()
+        gin_copy(r).wait()
+    pg_copy.wait()
 
 
 def paired_shards(
@@ -466,14 +520,20 @@
     taps = conv_weight.reshape(2, 3, 2, -1, hidden)
     taps_shape = taps.shape[2:]
     points_shape = (2, share // 2, channels)
-    copies = 5 * PIECES + 2 * CHUNKS + 6 + 3 * depth
-    vmem = pl.BlockSpec(memory_space=pltpu.VMEM)
+    copies = 6 * PIECES + 2 * CHUNKS + 6 + 3 * depth
     hbm = pl.BlockSpec(memory_space=pltpu.HBM)
     smem = pl.BlockSpec(memory_space=pltpu.SMEM)
     bf16, f32 = jnp.bfloat16, jnp.float32
     quarter = (share // 2, channels // 2)
     half = (share, channels // 2)
     scratch = [
+        pltpu.VMEM(in_gain.shape, f32),
+        pltpu.VMEM(in_gain.shape, f32),
+        pltpu.VMEM(mid_gain.shape, f32),
+        pltpu.VMEM(mid_gain.shape, f32),
+        pltpu.VMEM(point_weight.shape, bf16),
+        pltpu.VMEM((share, 2, channels), f32),
+        pltpu.VMEM((rows, channels), bf16),
         pltpu.VMEM((rows, channels), bf16),
         pltpu.VMEM((rows, channels), bf16),
         pltpu.VMEM((2,) + points_shape, bf16),
@@ -505,7 +565,7 @@
         pltpu.VMEM((2, depth) + quarter, bf16),
         pltpu.SemaphoreType.DMA((copies,)),
         pltpu.SemaphoreType.DMA((copies,)),
-        pltpu.SemaphoreType.DMA((2 + PIECES,)),
+        pltpu.SemaphoreType.DMA((8 + PIECES + CHUNKS,)),
     ]
     sample_count = sequence_in.shape[0] * lax.axis_size("dp")
     full_length = rows * lax.axis_size("seq")
@@ -516,11 +576,11 @@
             jax.ShapeDtypeStruct((share, 2, channels), f32),
             jax.ShapeDtypeStruct((rows, channels), bf16),
         ),
-        in_specs=[hbm, hbm, smem] + [vmem] * 4 + [hbm, vmem],
-        out_specs=(vmem, vmem),
+        in_specs=[hbm, hbm, smem] + [hbm] * 6,
+        out_specs=(hbm, hbm),
         scratch_shapes=scratch,
         compiler_params=pltpu.CompilerParams(
-            collective_id=0, has_side_effects=True, vmem_limit_bytes=48 * 2**20
+            collective_id=0, has_side_effects=True, vmem_limit_bytes=62 * 2**20
         ),
     )(
         sequence_in.reshape(rows, channels),

time: 67 us -> 57.4 us (0.86)
  local copies, waits for them, and re-layouts: 8.83 us -> 2.89 us
  Pallas kernels: 57.1 us -> 53.2 us
    unnamed x20 -> x4, local copies, waits for them, and re-layouts: 8.83 us -> 2.89 us
    pallas_call x1, Pallas kernels: 57.1 us -> 53.2 us  [paired_shards(): pl.pallas_call(functools.partial(paired_kernel, scale), out_shape=(jax.Sh...]
where the time goes in v3:
time: 57.4 us; the launch traced here: 56.7 us
  Pallas kernels  53.2 us (93%)
  local copies, waits for them, and re-layouts  2.89 us (5%)
  between operations  0.65 us (1%)
    pallas_call x1, Pallas kernels, paired_shards(): pl.pallas_call(functools.partial(paired_kernel, scale), out_shape=(jax.Sh...  53.2 us
    unnamed x4, local copies, waits for them, and re-layouts  2.89 us

profile of v3, /device:TPU:0, one launch (start us, length us, event | category | flops | bytes accessed | tf_op | source)
XLA Modules:
  0.0 56.7 jit_solution(3035998186458090016)
XLA Ops:
  0.6 53.2 %shard_map.104 = (f32[96,2,768]{2,1,0:T(2,128)}, bf16[512,768]{1,0:T(8,128)(2,1)}) custom-call(bf16[512,768]{1,0:T(8,128)(2,1)} %bitcast.6, bf16[512,768]{1,0:T(8,128)(2,1)} %bitcast.7, s32[1,2]{1,0:T(1,128)} %skip_ref.1, f32[2,768]{1,0:T(2,128)} %in_gain_hbm.1, f32[2,768]{1,0:T(2,128)} %in_shift_hbm.1, f32[2,384]{1,0:T(2,128)} %mid_gain_hbm.1, ...), custom_call_target="tpu_custom_call" | custom-call | tf_op jit(solution)/shard_map/pallas_call | solution.py:573
  53.8 0.0 copy-start
  53.9 2.0 %copy.13 = f32[96,2,768]{2,1,0:T(2,128)} copy(f32[96,2,768]{2,1,0:T(2,128)} %get-tuple-element.8) | data formatting | bytes 1179648
  55.9 0.0 copy-done
  55.9 0.9 %copy.14 = bf16[1,512,768]{2,1,0:T(8,128)(2,1)} copy(bf16[1,512,768]{2,1,0:T(8,128)(2,1)S(1)} %bitcast.5) | data formatting | bytes 1572864
Async XLA Ops:
  53.8 2.0 %copy-start = (bf16[512,768]{1,0:T(8,128)(2,1)S(1)}, bf16[512,768]{1,0:T(8,128)(2,1)}, u32[]{:S(2)}) copy-start(bf16[512,768]{1,0:T(8,128)(2,1)} %get-tuple-element.5) | copy-start | bytes 2359300

commit v4 on v3

--- a/solution.py
+++ b/solution.py
@@ -126,7 +126,6 @@
     act0,
     slope0,
     own_conv,
-    hidden_grad1,
     part_out,
     part_in,
     cgrad_out,
@@ -239,14 +238,16 @@
         other = place(k, far).at[1 - ypos]
         fwd_y.append(remote(other, other, 6 * k + 4, core_mate))
     own = [local(mine(k, False), place(k, seq), 7 + k) for k in range(PIECES)]
-    for k in range(PIECES):
-        if k == 2:
-            load_points.wait()
-            for b in range(2):
-                points[b] = pw_ref[:, b, :].reshape(points.shape[1:])
+
+    def send_piece(k):
         to_x[k].start()
         to_core[k].start()
         own[k].start()
+
+    send_piece(0)
+    load_points.wait()
+    for b in range(2):
+        points[b] = pw_ref[:, b, :].reshape(points.shape[1:])
 
     def after_x(k):
         to_x[k].wait_recv()
@@ -303,7 +304,11 @@
         slope0[spot, :] = slope * in_gain[0]
         bgrad1[spot, :] = (keep[1] * og_ref[spot, :].astype(jnp.float32)).astype(jnp.bfloat16)
 
-    chunked(start_block)
+    for r in range(CHUNKS):
+        send_piece(1 + r)
+        start_block(r)
+    for k in range(1 + CHUNKS, PIECES):
+        send_piece(k)
 
     part_base = 6 * PIECES
     cgrad_base = part_base + CHUNKS
@@ -326,11 +331,13 @@
         part_copy(r).start()
 
     chunked(make_part)
+    after_z(1)
     after_x(3)
+    after_z(2)
     after_x(4)
-    for k in range(1, PIECES):
-        after_z(k)
     after_y(1)
+    after_z(3)
+    after_z(4)
     ready(1)
 
     def make_own(r):
@@ -338,17 +345,8 @@
         own_conv[spot, :] = dot(act0[spot, :], conv_full(1))
 
     chunked(make_own)
-    for k in range(2, PIECES):
-        after_y(k)
-    ready(4)
-
-    def make_hidden_grad(r):
-        spot = at(r)
-        hidden_grad1[spot, :] = contract_last(bgrad1[spot, :], point_full(1))
-
-    chunked(make_hidden_grad)
+    after_y(2)
     ready(2)
-    ready(3)
 
     def middle_part(r):
         spot = at(r)
@@ -360,10 +358,17 @@
         branch = dot(act_hidden0, point_full(0))
         state = (x_ref[spot, :].astype(jnp.float32) + keep[0] * branch).astype(jnp.bfloat16)
         gelu, slope1 = gelu_and_slope(state.astype(jnp.float32) * in_gain[1] + in_shift[1])
+        if r == 0:
+            after_y(3)
+            ready(3)
         conv = dot(gelu.astype(jnp.bfloat16), conv_full(2))
         gelu, mid_slope1 = gelu_and_slope(conv * mid_gain[1] + mid_offset[1])
         hidden1[spot, :] = gelu.astype(jnp.bfloat16)
-        conv_grad = (mid_slope1 * hidden_grad1[spot, :] * mid_gain[1]).astype(jnp.bfloat16)
+        if r == 0:
+            after_y(4)
+            ready(4)
+        hidden_grad = contract_last(bgrad1[spot, :], point_full(1))
+        conv_grad = (mid_slope1 * hidden_grad * mid_gain[1]).astype(jnp.bfloat16)
         act_grad = contract_last(conv_grad, conv_full(2))
         gradient = (
             og_ref[spot, :].astype(jnp.float32) + slope1 * act_grad * in_gain[1]
@@ -477,17 +482,26 @@
     for copy in z_gather:
         copy.start()
     y_gather[0].start()
+
+    def settle(col, which):
+        block = final[col, which].astype(jnp.float32) * scale
+        for q in range(depth):
+            for side in range(2):
+
+                @pl.when((which == q) & (col == side))
+                def _():
+                    spot = slice((q % 2) * half_rows, (q % 2 + 1) * half_rows)
+                    pg_ref[spot, q // 2, side * half_cols : (side + 1) * half_cols] = block
+
+    settle(ypos, zpos)
     for j in range(1, depth):
         z_gather[j - 1].wait_recv()
         y_gather[j].start()
-    for copy in y_gather:
-        copy.wait_recv()
-    for b in range(2):
-        for part in range(2):
-            for col in range(2):
-                block = final[col, 2 * b + part].astype(jnp.float32) * scale
-                spot = slice(part * half_rows, (part + 1) * half_rows)
-                pg_ref[spot, b, col * half_cols : (col + 1) * half_cols] = block
+    for j in range(1, depth):
+        settle(ypos, (zpos + depth - j) % depth)
+    for j in range(depth):
+        y_gather[j].wait_recv()
+        settle(1 - ypos, (zpos + depth - j) % depth)
 
     pg_copy = local(pg_ref, pg_hbm, 7 + PIECES + CHUNKS)
     pg_copy.start()
@@ -500,6 +514,21 @@
         cgrad_copy(r).wait_send()
         gin_copy(r).wait()
     pg_copy.wait()
+
+
+def settle_kernel(pg_from, gin_from, pg_to, gin_to, sem):
+    copies = []
+    for index, (source, target) in enumerate(((pg_from, pg_to), (gin_from, gin_to))):
+        count = source.shape[0] // 4
+        for part in range(4):
+            spot = pl.ds(part * count, count)
+            copies.append(
+                pltpu.make_async_copy(source.at[spot], target.at[spot], sem.at[4 * index + part])
+            )
+    for copy in copies:
+        copy.start()
+    for copy in copies:
+        copy.wait()
 
 
 def paired_shards(
@@ -541,7 +570,6 @@
         pltpu.VMEM((2, 4) + points_shape, bf16),
         pltpu.VMEM((rows, channels), bf16),
         pltpu.VMEM((rows, channels), f32),
-        pltpu.VMEM((rows, hidden), f32),
         pltpu.VMEM((rows, hidden), f32),
         pltpu.VMEM((rows, hidden), bf16),
         pltpu.VMEM((rows, hidden), bf16),
@@ -593,6 +621,17 @@
         taps,
         point_weight,
     )
+    point_grad, gradient = pl.pallas_call(
+        settle_kernel,
+        out_shape=(
+            jax.ShapeDtypeStruct(point_grad.shape, f32),
+            jax.ShapeDtypeStruct(gradient.shape, bf16),
+        ),
+        in_specs=[hbm, hbm],
+        out_specs=(hbm, hbm),
+        scratch_shapes=[pltpu.SemaphoreType.DMA((8,))],
+        compiler_params=pltpu.CompilerParams(vmem_limit_bytes=62 * 2**20),
+    )(point_grad, gradient)
     return (point_grad, gradient.reshape(sequence_in.shape))
 
 

time: 57.4 us -> 98 us (1.71)
  Pallas kernels: 53.2 us -> 97.2 us
  local copies, waits for them, and re-layouts: 2.89 us -> 0 us
    pallas_call x0 -> x1, Pallas kernels: none -> 42.9 us  [paired_shards(): pl.pallas_call(settle_kernel, out_shape=(jax.ShapeDtypeStruct(point_grad....]
    unnamed x4 -> x0, local copies, waits for them, and re-layouts: 2.89 us -> none
    pallas_call x1, Pallas kernels: 53.2 us -> 54.3 us  [paired_shards(): pl.pallas_call(functools.partial(paired_kernel, scale), out_shape=(jax.Sh...]
where the time goes in v4:
time: 98 us; the launch traced here: 97.8 us
  Pallas kernels  97.2 us (99%)
    pallas_call x1, Pallas kernels, paired_shards(): pl.pallas_call(functools.partial(paired_kernel, scale), out_shape=(jax.Sh...  54.3 us
    pallas_call x1, Pallas kernels, paired_shards(): pl.pallas_call(settle_kernel, out_shape=(jax.ShapeDtypeStruct(point_grad....  42.9 us

profile of v4, /device:TPU:0, one launch (start us, length us, event | category | flops | bytes accessed | tf_op | source)
XLA Modules:
  0.0 97.8 jit_solution(14453356611679531315)
XLA Ops:
  0.6 54.3 %shard_map.104 = (f32[96,2,768]{2,1,0:T(2,128)}, bf16[512,768]{1,0:T(8,128)(2,1)}) custom-call(bf16[512,768]{1,0:T(8,128)(2,1)} %bitcast.5, bf16[512,768]{1,0:T(8,128)(2,1)} %bitcast.6, s32[1,2]{1,0:T(1,128)} %skip_ref.1, f32[2,768]{1,0:T(2,128)} %in_gain_hbm.1, f32[2,768]{1,0:T(2,128)} %in_shift_hbm.1, f32[2,384]{1,0:T(2,128)} %mid_gain_hbm.1, ...), custom_call_target="tpu_custom_call" | custom-call | tf_op jit(solution)/shard_map/pallas_call | solution.py:601
  54.9 42.9 %shard_map.105 = (f32[96,2,768]{2,1,0:T(2,128)}, bf16[512,768]{1,0:T(8,128)(2,1)}) custom-call(f32[96,2,768]{2,1,0:T(2,128)} %get-tuple-element.6.pg_from, bf16[512,768]{1,0:T(8,128)(2,1)} %get-tuple-element.7.gin_from), custom_call_target="tpu_custom_call" | custom-call | tf_op jit(solution)/shard_map/pallas_call | solution.py:624

commit v5 on v4

--- a/solution.py
+++ b/solution.py
@@ -76,6 +76,7 @@
 MESH = pl.DeviceIdType.MESH
 CHUNKS = 2
 PIECES = 5
+THROUGH_Z = (3, 4)
 TANH_SCALE = 0.7978845608028654
 CUBIC = 0.044715
 
@@ -219,20 +220,21 @@
         count = half.shape[1] // 2
         return half.at[:, pl.ds(pl.multiple_of(which * count, count), count)]
 
-    to_core, to_x, to_z, to_y, fwd_x, fwd_y = [], [], [], [], [], []
+    to_core, to_x, to_y, fwd_x, fwd_y = [], [], [], [], []
+    to_z = {}
     for k in range(PIECES):
         to_core.append(remote(mine(k, False), place(k, seq), 6 * k, core_mate))
         if k == 0:
             to_x.append(remote(mine(k, True), place(k, seq), 1, x_mate))
             fwd_x.append(remote(place(k, far), place(k, far), 3, core_mate))
             continue
-        near_quarter = quarter_of(mine(k, True).at[ypos], zlow)
-        to_x.append(
-            remote(near_quarter, quarter_of(place(k, seq).at[ypos], zlow), 6 * k + 1, x_mate)
-        )
         half = place(k, far).at[ypos]
-        quarter = quarter_of(half, zlow)
-        to_z.append(remote(quarter, quarter, 6 * k + 5, z_near))
+        mine_half, there = mine(k, True).at[ypos], place(k, seq).at[ypos]
+        if k in THROUGH_Z:
+            mine_half, there = quarter_of(mine_half, zlow), quarter_of(there, zlow)
+            quarter = quarter_of(half, zlow)
+            to_z[k] = remote(quarter, quarter, 6 * k + 5, z_near)
+        to_x.append(remote(mine_half, there, 6 * k + 1, x_mate))
         to_y.append(remote(half, half, 6 * k + 2, y_mate))
         fwd_x.append(remote(half, half, 6 * k + 3, core_mate))
         other = place(k, far).at[1 - ypos]
@@ -245,19 +247,24 @@
         own[k].start()
 
     send_piece(0)
+    send_piece(1)
     load_points.wait()
     for b in range(2):
         points[b] = pw_ref[:, b, :].reshape(points.shape[1:])
+    for k in range(2, PIECES):
+        send_piece(k)
 
     def after_x(k):
         to_x[k].wait_recv()
-        if k == 0:
-            fwd_x[0].start()
-        else:
-            to_z[k - 1].start()
+        if k in THROUGH_Z:
+            to_z[k].start()
+            return
+        fwd_x[k].start()
+        if k > 0:
+            to_y[k - 1].start()
 
     def after_z(k):
-        to_z[k - 1].wait_recv()
+        to_z[k].wait_recv()
         to_y[k - 1].start()
         fwd_x[k].start()
 
@@ -299,16 +306,15 @@
     def start_block(r):
         spot = at(r)
         value = x_ref[spot, :].astype(jnp.float32) * in_gain[0] + in_shift[0]
-        gelu, slope = gelu_and_slope(value)
-        act0[spot, :] = gelu.astype(jnp.bfloat16)
-        slope0[spot, :] = slope * in_gain[0]
+        act0[spot, :] = gelu_only(value).astype(jnp.bfloat16)
+
+    def start_slopes(r):
+        spot = at(r)
+        value = x_ref[spot, :].astype(jnp.float32) * in_gain[0] + in_shift[0]
+        slope0[spot, :] = gelu_and_slope(value)[1] * in_gain[0]
         bgrad1[spot, :] = (keep[1] * og_ref[spot, :].astype(jnp.float32)).astype(jnp.bfloat16)
 
-    for r in range(CHUNKS):
-        send_piece(1 + r)
-        start_block(r)
-    for k in range(1 + CHUNKS, PIECES):
-        send_piece(k)
+    chunked(start_block)
 
     part_base = 6 * PIECES
     cgrad_base = part_base + CHUNKS
@@ -322,7 +328,6 @@
 
     after_x(0)
     after_x(1)
-    after_x(2)
     ready(0)
 
     def make_part(r):
@@ -331,13 +336,14 @@
         part_copy(r).start()
 
     chunked(make_part)
-    after_z(1)
+    after_x(2)
     after_x(3)
-    after_z(2)
     after_x(4)
     after_y(1)
     after_z(3)
     after_z(4)
+    after_y(2)
+    chunked(start_slopes)
     ready(1)
 
     def make_own(r):
@@ -345,7 +351,6 @@
         own_conv[spot, :] = dot(act0[spot, :], conv_full(1))
 
     chunked(make_own)
-    after_y(2)
     ready(2)
 
     def middle_part(r):
@@ -506,7 +511,7 @@
     pg_copy = local(pg_ref, pg_hbm, 7 + PIECES + CHUNKS)
     pg_copy.start()
     sums = (core_copy, one_copy, two_copy, z_copy, z_gather, y_gather)
-    for group in (to_core, to_x, to_z, to_y, fwd_x, fwd_y) + sums:
+    for group in (to_core, to_x, to_z.values(), to_y, fwd_x, fwd_y) + sums:
         for copy in group:
             copy.wait_send()
     for r in range(CHUNKS):
@@ -516,19 +521,22 @@
     pg_copy.wait()
 
 
-def settle_kernel(pg_from, gin_from, pg_to, gin_to, sem):
-    copies = []
-    for index, (source, target) in enumerate(((pg_from, pg_to), (gin_from, gin_to))):
-        count = source.shape[0] // 4
+def settle_kernel(pg_from, gin_from, pg_to, gin_to, pg_ref, gin_ref, sem):
+    ways = []
+    for index, refs in enumerate(((pg_from, pg_ref, pg_to), (gin_from, gin_ref, gin_to))):
+        count = refs[0].shape[0] // 4
         for part in range(4):
-            spot = pl.ds(part * count, count)
-            copies.append(
-                pltpu.make_async_copy(source.at[spot], target.at[spot], sem.at[4 * index + part])
-            )
-    for copy in copies:
-        copy.start()
-    for copy in copies:
-        copy.wait()
+            source, middle, target = [ref.at[pl.ds(part * count, count)] for ref in refs]
+            spot = 8 * index + 2 * part
+            fetch = pltpu.make_async_copy(source, middle, sem.at[spot])
+            ways.append((fetch, pltpu.make_async_copy(middle, target, sem.at[spot + 1])))
+    for fetch, _ in ways:
+        fetch.start()
+    for fetch, store in ways:
+        fetch.wait()
+        store.start()
+    for _, store in ways:
+        store.wait()
 
 
 def paired_shards(
@@ -629,7 +637,11 @@
         ),
         in_specs=[hbm, hbm],
         out_specs=(hbm, hbm),
-        scratch_shapes=[pltpu.SemaphoreType.DMA((8,))],
+        scratch_shapes=[
+            pltpu.VMEM(point_grad.shape, f32),
+            pltpu.VMEM(gradient.shape, bf16),
+            pltpu.SemaphoreType.DMA((16,)),
+        ],
         compiler_params=pltpu.CompilerParams(vmem_limit_bytes=62 * 2**20),
     )(point_grad, gradient)
     return (point_grad, gradient.reshape(sequence_in.shape))

time: 98 us -> 55.7 us (0.57)
  Pallas kernels: 97.2 us -> 54.9 us
    pallas_call x1, Pallas kernels: 42.9 us -> 2.23 us  [paired_shards(): pl.pallas_call(settle_kernel, out_shape=(jax.ShapeDtypeStruct(point_grad....]
    pallas_call x1, Pallas kernels: 54.3 us -> 52.7 us  [paired_shards(): pl.pallas_call(functools.partial(paired_kernel, scale), out_shape=(jax.Sh...]
where the time goes in v5:
time: 55.7 us; the launch traced here: 55.6 us
  Pallas kernels  54.9 us (99%)
  between operations  0.64 us (1%)
    pallas_call x1, Pallas kernels, paired_shards(): pl.pallas_call(functools.partial(paired_kernel, scale), out_shape=(jax.Sh...  52.7 us
    pallas_call x1, Pallas kernels, paired_shards(): pl.pallas_call(settle_kernel, out_shape=(jax.ShapeDtypeStruct(point_grad....  2.23 us

profile of v5, /device:TPU:0, one launch (start us, length us, event | category | flops | bytes accessed | tf_op | source)
XLA Modules:
  0.0 55.6 jit_solution(11791043057662859886)
XLA Ops:
  0.6 52.7 %shard_map.104 = (f32[96,2,768]{2,1,0:T(2,128)}, bf16[512,768]{1,0:T(8,128)(2,1)}) custom-call(bf16[512,768]{1,0:T(8,128)(2,1)} %bitcast.5, bf16[512,768]{1,0:T(8,128)(2,1)} %bitcast.6, s32[1,2]{1,0:T(1,128)} %skip_ref.1, f32[2,768]{1,0:T(2,128)} %in_gain_hbm.1, f32[2,768]{1,0:T(2,128)} %in_shift_hbm.1, f32[2,384]{1,0:T(2,128)} %mid_gain_hbm.1, ...), custom_call_target="tpu_custom_call" | custom-call | tf_op jit(solution)/shard_map/pallas_call | solution.py:609
  53.3 2.2 %shard_map.105 = (f32[96,2,768]{2,1,0:T(2,128)}, bf16[512,768]{1,0:T(8,128)(2,1)}) custom-call(f32[96,2,768]{2,1,0:T(2,128)} %get-tuple-element.6.pg_from, bf16[512,768]{1,0:T(8,128)(2,1)} %get-tuple-element.7.gin_from), custom_call_target="tpu_custom_call" | custom-call | tf_op jit(solution)/shard_map/pallas_call | solution.py:632

commit v6 on v5

--- a/solution.py
+++ b/solution.py
@@ -100,7 +100,6 @@
 
 
 def paired_kernel(
-    scale,
     x_hbm,
     og_hbm,
     skip_ref,
@@ -117,7 +116,6 @@
     mid_gain_ref,
     mid_offset_ref,
     pw_ref,
-    pg_ref,
     gin_ref,
     x_ref,
     og_ref,
@@ -478,7 +476,6 @@
             z_out[2 * b + part] = block.astype(jnp.bfloat16)
     for copy in z_copy:
         copy.start()
-    last_part(1)
     total = z_keep[zpos]
     for j in range(1, depth):
         z_copy[j - 1].wait_recv()
@@ -488,28 +485,22 @@
         copy.start()
     y_gather[0].start()
 
-    def settle(col, which):
-        block = final[col, which].astype(jnp.float32) * scale
-        for q in range(depth):
-            for side in range(2):
-
-                @pl.when((which == q) & (col == side))
-                def _():
-                    spot = slice((q % 2) * half_rows, (q % 2 + 1) * half_rows)
-                    pg_ref[spot, q // 2, side * half_cols : (side + 1) * half_cols] = block
-
-    settle(ypos, zpos)
+    def store_piece(col, which, index):
+        copy = local(final.at[col, which], pg_hbm.at[col, which], 7 + PIECES + CHUNKS + index)
+        copy.start()
+        return copy
+
+    last_part(1)
+    stored = [store_piece(ypos, zpos, 0)]
     for j in range(1, depth):
         z_gather[j - 1].wait_recv()
         y_gather[j].start()
     for j in range(1, depth):
-        settle(ypos, (zpos + depth - j) % depth)
+        stored.append(store_piece(ypos, (zpos + depth - j) % depth, j))
     for j in range(depth):
         y_gather[j].wait_recv()
-        settle(1 - ypos, (zpos + depth - j) % depth)
-
-    pg_copy = local(pg_ref, pg_hbm, 7 + PIECES + CHUNKS)
-    pg_copy.start()
+        stored.append(store_piece(1 - ypos, (zpos + depth - j) % depth, depth + j))
+
     sums = (core_copy, one_copy, two_copy, z_copy, z_gather, y_gather)
     for group in (to_core, to_x, to_z.values(), to_y, fwd_x, fwd_y) + sums:
         for copy in group:
@@ -518,24 +509,39 @@
         part_copy(r).wait_send()
         cgrad_copy(r).wait_send()
         gin_copy(r).wait()
-    pg_copy.wait()
-
-
-def settle_kernel(pg_from, gin_from, pg_to, gin_to, pg_ref, gin_ref, sem):
+    for copy in stored:
+        copy.wait()
+
+
+def settle_kernel(scale, sum_from, gin_from, pg_to, gin_to, sum_ref, pg_ref, gin_ref, sem):
+    fetch_sum = pltpu.make_async_copy(sum_from, sum_ref, sem.at[0])
+    fetch_sum.start()
+    count = gin_from.shape[0] // 4
     ways = []
-    for index, refs in enumerate(((pg_from, pg_ref, pg_to), (gin_from, gin_ref, gin_to))):
-        count = refs[0].shape[0] // 4
-        for part in range(4):
-            source, middle, target = [ref.at[pl.ds(part * count, count)] for ref in refs]
-            spot = 8 * index + 2 * part
-            fetch = pltpu.make_async_copy(source, middle, sem.at[spot])
-            ways.append((fetch, pltpu.make_async_copy(middle, target, sem.at[spot + 1])))
-    for fetch, _ in ways:
+    for part in range(4):
+        source, middle, target = [
+            ref.at[pl.ds(part * count, count)] for ref in (gin_from, gin_ref, gin_to)
+        ]
+        fetch = pltpu.make_async_copy(source, middle, sem.at[1 + part])
         fetch.start()
+        ways.append((fetch, pltpu.make_async_copy(middle, target, sem.at[5 + part])))
+    fetch_sum.wait()
+    rows, cols = sum_ref.shape[2:]
+    stores = []
+    for part in range(2):
+        for b in range(2):
+            for col in range(2):
+                block = sum_ref[col, 2 * b + part].astype(jnp.float32) * scale
+                spot = slice(part * rows, (part + 1) * rows)
+                pg_ref[spot, b, col * cols : (col + 1) * cols] = block
+        spot = pl.ds(part * rows, rows)
+        stores.append(pltpu.make_async_copy(pg_ref.at[spot], pg_to.at[spot], sem.at[9 + part]))
+        stores[-1].start()
     for fetch, store in ways:
         fetch.wait()
         store.start()
-    for _, store in ways:
+        stores.append(store)
+    for store in stores:
         store.wait()
 
 
@@ -569,7 +575,6 @@
         pltpu.VMEM(mid_gain.shape, f32),
         pltpu.VMEM(mid_gain.shape, f32),
         pltpu.VMEM(point_weight.shape, bf16),
-        pltpu.VMEM((share, 2, channels), f32),
         pltpu.VMEM((rows, channels), bf16),
         pltpu.VMEM((rows, channels), bf16),
         pltpu.VMEM((rows, channels), bf16),
@@ -601,15 +606,15 @@
         pltpu.VMEM((2, depth) + quarter, bf16),
         pltpu.SemaphoreType.DMA((copies,)),
         pltpu.SemaphoreType.DMA((copies,)),
-        pltpu.SemaphoreType.DMA((8 + PIECES + CHUNKS,)),
+        pltpu.SemaphoreType.DMA((7 + PIECES + CHUNKS + 2 * depth,)),
     ]
     sample_count = sequence_in.shape[0] * lax.axis_size("dp")
     full_length = rows * lax.axis_size("seq")
     scale = 1.0 / math.sqrt(sample_count * full_length)
-    point_grad, gradient = pl.pallas_call(
-        functools.partial(paired_kernel, scale),
+    summed, gradient = pl.pallas_call(
+        paired_kernel,
         out_shape=(
-            jax.ShapeDtypeStruct((share, 2, channels), f32),
+            jax.ShapeDtypeStruct((2, depth) + quarter, bf16),
             jax.ShapeDtypeStruct((rows, channels), bf16),
         ),
         in_specs=[hbm, hbm, smem] + [hbm] * 6,
@@ -630,20 +635,21 @@
         point_weight,
     )
     point_grad, gradient = pl.pallas_call(
-        settle_kernel,
+        functools.partial(settle_kernel, scale),
         out_shape=(
-            jax.ShapeDtypeStruct(point_grad.shape, f32),
+            jax.ShapeDtypeStruct((share, 2, channels), f32),
             jax.ShapeDtypeStruct(gradient.shape, bf16),
         ),
         in_specs=[hbm, hbm],
         out_specs=(hbm, hbm),
         scratch_shapes=[
-            pltpu.VMEM(point_grad.shape, f32),
+            pltpu.VMEM(summed.shape, bf16),
+            pltpu.VMEM((share, 2, channels), f32),
             pltpu.VMEM(gradient.shape, bf16),
-            pltpu.SemaphoreType.DMA((16,)),
+            pltpu.SemaphoreType.DMA((11,)),
         ],
         compiler_params=pltpu.CompilerParams(vmem_limit_bytes=62 * 2**20),
-    )(point_grad, gradient)
+    )(summed, gradient)
     return (point_grad, gradient.reshape(sequence_in.shape))
 
 

time: 55.7 us -> 55.5 us (level)
  no operation moved by 1% of the time
where the time goes in v6:
time: 55.5 us; the launch traced here: 55.3 us
  Pallas kernels  54.7 us (99%)
  between operations  0.64 us (1%)
    pallas_call x1, Pallas kernels, paired_shards(): pl.pallas_call(paired_kernel, out_shape=(jax.ShapeDtypeStruct((2, depth)...  52.5 us
    pallas_call x1, Pallas kernels, paired_shards(): pl.pallas_call(functools.partial(settle_kernel, scale), out_shape=(jax.Sh...  2.21 us

profile of v6, /device:TPU:0, one launch (start us, length us, event | category | flops | bytes accessed | tf_op | source)
XLA Modules:
  0.0 55.3 jit_solution(4457290615558904331)
XLA Ops:
  0.6 52.5 %shard_map.104 = (bf16[2,4,48,384]{3,2,1,0:T(8,128)(2,1)}, bf16[512,768]{1,0:T(8,128)(2,1)}) custom-call(bf16[512,768]{1,0:T(8,128)(2,1)} %bitcast.5, bf16[512,768]{1,0:T(8,128)(2,1)} %bitcast.6, s32[1,2]{1,0:T(1,128)} %skip_ref.1, f32[2,768]{1,0:T(2,128)} %in_gain_hbm.1, f32[2,768]{1,0:T(2,128)} %in_shift_hbm.1, f32[2,384]{1,0:T(2,128)} %mid_gain_hbm.1, ...), custom_call_target="tpu_custom_call" | custom-call | tf_op jit(solution)/shard_map/pallas_call | solution.py:614
  53.1 2.2 %shard_map.105 = (f32[96,2,768]{2,1,0:T(2,128)}, bf16[512,768]{1,0:T(8,128)(2,1)}) custom-call(bf16[2,4,48,384]{3,2,1,0:T(8,128)(2,1)} %get-tuple-element.6.sum_from, bf16[512,768]{1,0:T(8,128)(2,1)} %get-tuple-element.7.gin_from), custom_call_target="tpu_custom_call" | custom-call | tf_op jit(solution)/shard_map/pallas_call | solution.py:637
